TPU v7x, 32 devices: a whole 2x2x4 slice. The times are simulated.
32 devices in a mesh: group: 2 (over x), mp: 16 (over z, y, core).
Axes of the slice: x: 2, y: 2, z: 4, core: 2. Of those that a mesh axis runs over, the one named last changes fastest.
Arguments:
- tokens: bfloat16 [4096, 8192], P(('group', 'mp')), parts along dimension 0, may hold values from -6 to 6
- norm_gain: float32 [8192], replicated, may hold values from 0.5 to 2
- query_tiles: bfloat16 [32768, 2048], P('mp'), may hold values from -0.0625 to 0.0625
- key_weight_tiles: bfloat16 [32768, 256], P('mp'), may hold values from -0.0625 to 0.0625
- value_weight_tiles: bfloat16 [32768, 256], P('mp'), may hold values from -0.0625 to 0.0625
- output_tiles: bfloat16 [32768, 2048], P('mp'), may hold values from -0.25 to 0.25
- visits: int32 [8, 512], P('group'), parts along dimension 0, may hold values from 0 to 31, as said below
- lengths: int32 [8], P('group'), parts along dimension 0, may hold values from 128 to 512, as said below
Outputs:
- attended: bfloat16 [4096, 8192], P(('group', 'mp')), parts along dimension 0
There are 2 independent parts, one for each index of `group`. A program takes and returns all parts, laid end to end along the dimension named above; an argument that names none is the same for every part. Nothing has to cross between parts.
Inputs may be any that keep to these rules, and one draw needn't show every extreme that they name: `visits`: each row starts at 0, rises by 0 or 1 from one token to the next, and ends at 31. `lengths`: one timeline of each part has all 512 tokens real.
All inputs are finite; a program needn't handle non-finite values.
Results may differ from a plain program's by a relative error of at most 0.012.
Values may be sent and summed in bfloat16 or wider, within the bound.
A program may use at most 320 MiB of HBM per device.

v0:
```python
import jax
import jax.numpy as jnp
from jax import lax
from jax.sharding import PartitionSpec as P

KEY_VALUE_HEADS = 8
HEAD_SIZE = 128
PART_TIMELINES = 4


def partner_2(value, axis, bit):
    mask = 2**bit
    pairs = [(source, source ^ mask) for source in range(lax.axis_size(axis))]
    return lax.ppermute(value, axis, pairs)


def upper_half(device_index, bit_number):
    return device_index // (1 << bit_number) % 2 == 1


def joined(current, partner, partner_first, axis_number):
    lower = jnp.where(partner_first, partner, current)
    higher = jnp.where(partner_first, current, partner)
    return jnp.concatenate([lower, higher], axis=axis_number)


def butterfly(pieces, device_index, bit_count, mover):
    count = pieces.shape[0]
    rest = pieces.shape[1:]
    for bit_number in range(bit_count):
        split = pieces.reshape((count >> bit_number + 1, 2, 1 << bit_number) + rest)
        upper_side = upper_half(device_index, bit_number)
        kept = jnp.where(upper_side, split[:, 1], split[:, 0])
        given = jnp.where(upper_side, split[:, 0], split[:, 1])
        arrived = mover(given, bit_number)
        lower = jnp.where(upper_side, arrived, kept)
        higher = jnp.where(upper_side, kept, arrived)
        pieces = jnp.stack([lower, higher], axis=1).reshape((count,) + rest)
    return pieces


def rotary_embedding(value_rows):
    positions = jnp.arange(value_rows.shape[0], dtype=jnp.float32)
    half_width = value_rows.shape[-1] // 2
    inverse = jnp.power(
        500000.0, -jnp.arange(half_width, dtype=jnp.float32) * 2.0 / value_rows.shape[-1]
    )
    angles = positions[:, None, None] * inverse[None, None, :]
    cosine = jnp.cos(angles)
    sine = jnp.sin(angles)
    first = value_rows[..., :half_width]
    second = value_rows[..., half_width:]
    return jnp.concatenate(
        [first * cosine - second * sine, second * cosine + first * sine], axis=-1
    )


def shards(
    tokens,
    norm_gain,
    query_tiles,
    key_weight_tiles,
    value_weight_tiles,
    output_tiles,
    visits,
    lengths,
):
    query_head_groups = lax.axis_size("mp") // PART_TIMELINES
    group_bits = query_head_groups.bit_length() - 1
    timeline_bits = PART_TIMELINES.bit_length() - 1
    device_index = lax.axis_index("mp")
    timeline = device_index // query_head_groups
    widened = tokens.astype(jnp.float32)
    normed = (
        widened * lax.rsqrt(jnp.mean(widened * widened, axis=1, keepdims=True) + 1e-05) * norm_gain
    ).astype(jnp.bfloat16)
    gathered = normed
    for bit_number in range(group_bits):
        partner = partner_2(gathered, "mp", bit_number)
        gathered = joined(gathered, partner, upper_half(device_index, bit_number), 0)
    query_weight = query_tiles
    for section_number in range(timeline_bits):
        bit_number = group_bits + section_number
        partner = partner_2(query_weight, "mp", bit_number)
        query_weight = joined(query_weight, partner, upper_half(device_index, bit_number), 0)
    head_repeats = max(1, query_head_groups // KEY_VALUE_HEADS)
    repeat_bits = head_repeats.bit_length() - 1
    stacked = jnp.stack([key_weight_tiles, value_weight_tiles])
    roster = [(group_bits + section_number, 1) for section_number in range(timeline_bits)]
    roster = roster + [(section_number, 2) for section_number in range(repeat_bits)]
    for bit_number, axis_number in roster:
        partner = partner_2(stacked, "mp", bit_number)
        stacked = joined(stacked, partner, upper_half(device_index, bit_number), axis_number)
    projected = jnp.einsum("td,sdc->stc", gathered, stacked, preferred_element_type=jnp.float32)
    timeline_rows = gathered.shape[0]
    key_rows = rotary_embedding(projected[0].reshape(timeline_rows, -1, HEAD_SIZE)).astype(
        jnp.bfloat16
    )
    value_rows = projected[1].astype(jnp.bfloat16).reshape(timeline_rows, -1, HEAD_SIZE)
    local_kv = key_rows.shape[1]
    query_vectors = jnp.dot(gathered, query_weight, preferred_element_type=jnp.float32).reshape(
        timeline_rows, -1, HEAD_SIZE
    )
    local_heads = query_vectors.shape[1]
    query_vectors = (
        (rotary_embedding(query_vectors) * HEAD_SIZE ** (-0.5))
        .astype(jnp.bfloat16)
        .reshape(timeline_rows, local_kv, local_heads // local_kv, HEAD_SIZE)
    )
    visit_row = lax.dynamic_index_in_dim(visits, timeline, 0, keepdims=False)
    real_count = lax.dynamic_index_in_dim(lengths, timeline, 0, keepdims=False)
    positions = jnp.arange(timeline_rows, dtype=jnp.int32)
    allowed = (visit_row[None, :] <= visit_row[:, None]) & (positions[None, :] < real_count)
    scores = jnp.einsum(
        "qhgd,khd->hgqk", query_vectors, key_rows, preferred_element_type=jnp.float32
    )
    raw_weights = jnp.where(allowed, jnp.exp(scores), 0.0)
    probs = (raw_weights / jnp.sum(raw_weights, axis=-1, keepdims=True)).astype(jnp.bfloat16)
    heads = (
        jnp.einsum("hgqk,khd->qhgd", probs, value_rows, preferred_element_type=jnp.float32)
        .astype(jnp.bfloat16)
        .reshape(timeline_rows, -1)
    )
    owned = tokens.shape[0]
    all_heads = heads
    for bit_number in range(group_bits):
        partner = partner_2(all_heads, "mp", bit_number)
        all_heads = joined(all_heads, partner, upper_half(device_index, bit_number), 1)
    tile_rows = output_tiles.shape[0]
    blocks = output_tiles.reshape(tile_rows, query_head_groups, -1).transpose(1, 0, 2)

    def move_blocks(given, bit_number):
        return partner_2(given, "mp", bit_number)

    blocks = butterfly(blocks, device_index, group_bits, move_blocks)
    narrow = blocks.shape[2]
    column_weight = blocks.reshape(query_head_groups * tile_rows, narrow)
    for section_number in range(timeline_bits):
        bit_number = group_bits + section_number
        partner = partner_2(column_weight, "mp", bit_number)
        column_weight = joined(column_weight, partner, upper_half(device_index, bit_number), 1)
    finished = jnp.dot(all_heads, column_weight, preferred_element_type=jnp.float32).astype(
        jnp.bfloat16
    )
    outgoing = finished.reshape(query_head_groups, owned, PART_TIMELINES * narrow)

    def move_rows(given, bit_number):
        return partner_2(given, "mp", bit_number)

    incoming = butterfly(outgoing, device_index, group_bits, move_rows)
    incoming = incoming.reshape(query_head_groups, owned, PART_TIMELINES, narrow).transpose(
        1, 2, 0, 3
    )
    return incoming.reshape(owned, PART_TIMELINES * query_head_groups * narrow)


def solution(mesh):
    return jax.shard_map(
        shards,
        mesh=mesh,
        in_specs=(
            P(("group", "mp"), None),
            P(),
            P("mp", None),
            P("mp", None),
            P("mp", None),
            P("mp", None),
            P("group", None),
            P("group"),
        ),
        out_specs=P(("group", "mp"), None),
        check_vma=False,
    )
```

profile of v0, /device:TPU:0, one launch (start us, length us, event | category | flops | bytes accessed | tf_op | source)
XLA Modules:
  0.0 2029.0 jit_solution(14245579220502984156)
XLA Ops:
  0.0 3.0 collective-permute-start.4
  3.0 12.3 copy.72
  15.3 11.4 copy.73
  26.7 5.1 select_bitcast_fusion.1
  31.8 1.6 copy.65
  33.5 2.3 copy.66
  35.8 2.7 pad_maximum_fusion.11
  38.6 0.5 fusion.18
  39.1 1.9 fusion.20
  41.0 0.3 collective-permute-start.2
  41.3 187.5 %collective-permute-done = bf16[2,2048,256]{1,2,0:T(8,128)(2,1)} collective-permute-done((bf16[2,2048,256]{1,2,0:T(8,128)(2,1)}, bf16[2,2048,256]{1,2,0:T(8,128)(2,1)}, u32[]{:S(2)}, u32[]{:S(2)}) %collective-permute-start) | collective-permute-done | bytes 2097184 | tf_op jit(solution)/shard_map/ppermute | solution.py:14
  228.7 3.6 broadcast_select_fusion.19
  232.4 8.9 fusion.24
  241.2 7.5 maximum_bitcast_fusion
  248.7 3.7 select_bitcast_fusion
  252.4 1.8 collective-permute-start.9
  254.2 6.5 broadcast_select_fusion.7
  260.7 7.7 pad_maximum_fusion
  268.5 0.8 copy-done.2
  269.3 2.5 copy-done.3
  271.8 2.6 collective-permute-start.5
  274.4 2.5 pad_maximum_fusion.6
  276.9 0.3 collective-permute-start.1
  277.3 4.5 broadcast_select_fusion.17
  281.8 62.5 %collective-permute-done.9 = bf16[1,2,2048,512]{3,2,1,0:T(8,128)(2,1)S(1)} collective-permute-done((bf16[1,2,2048,512]{3,2,1,0:T(8,128)(2,1)S(1)}, bf16[1,2,2048,512]{3,2,1,0:T(8,128)(2,1)S(1)}, u32[]{:S(2)}, u32[]{:S(2)}) %collective-permute-start.9) | collective-permute-done | bytes 4194336 | tf_op jit(solution)/shard_map/ppermute | solution.py:14
  344.3 3.6 fusion.22
  347.9 7.6 pad_maximum_fusion.3
  355.5 1.4 collective-permute-start.10
  357.0 2.3 pad_maximum_fusion.7
  359.2 1.5 collective-permute-start.3
  360.8 0.6 dynamic_slice.9
  361.4 0.7 iota_compare_fusion
  362.3 1.0 fusion.50
  363.3 809.8 %collective-permute-done.1 = bf16[2,4096,256]{1,2,0:T(8,128)(2,1)} collective-permute-done((bf16[2,4096,256]{1,2,0:T(8,128)(2,1)}, bf16[2,4096,256]{1,2,0:T(8,128)(2,1)}, u32[]{:S(2)}, u32[]{:S(2)}) %collective-permute-start.1) | collective-permute-done | bytes 4194336 | tf_op jit(solution)/shard_map/ppermute | solution.py:14
  1173.1 6.6 broadcast_select_fusion.13
  1179.7 6.0 broadcast_select_fusion.11
  1185.8 10.4 fusion.38
  1196.2 0.7 slice.132
  1197.5 6.5 broadcast_select_fusion.5
  1204.0 10.1 pad_maximum_fusion.1
  1214.1 0.8 copy-done.5
  1214.9 24.4 %broadcast_select_fusion.3 = (bf16[4096,2048]{1,0:T(8,128)(2,1)}, bf16[4096,2048]{1,0:T(8,128)(2,1)}) fusion(bf16[4096,2048]{1,0:T(8,128)(2,1)} %collective-permute-done.5, pred[]{:T(512)S(6)} %eq.39, bf16[2048,2048]{1,0:T(8,128)(2,1)} %copy-done.3, bf16[2048,2048]{1,0:T(8,128)(2,1)} %copy-done.2), kind=kLoop, calls=%fused_computation.15 | loop fusion | flops 50331648 | bytes 67108864 | tf_op jit(solution)/shard_map/jit(_where)/select_n | solution.py:22
  1239.3 24.9 %fusion.31 = f32[64,8,16,128]{3,1,2,0:T(8,128)} fusion(bf16[4096,2048]{1,0:T(8,128)(2,1)} %get-tuple-element.6, bf16[4096,2048]{1,0:T(8,128)(2,1)} %get-tuple-element.5, bf16[256,8192]{1,0:T(8,128)(2,1)} %get-tuple-element.22, bf16[256,8192]{1,0:T(8,128)(2,1)} %get-tuple-element.21), kind=kOutput, calls=%fused_computation.64 | convolution fusion | flops 17263755264 | bytes 46137344 | tf_op jit(solution)/shard_map/dot_general | solution.py:101
  1264.3 3.1 copy.90
  1267.4 1.7 multiply_subtract_fusion
  1269.1 1.4 copy.69
  1270.4 3.2 copy.70
  1273.7 6.2 fusion.8
  1279.9 4.0 fusion.37
  1284.0 4.1 collective-permute-done.6
  1288.1 0.4 broadcast_select_fusion.21
  1288.5 0.3 pad_maximum_fusion.8
  1288.8 0.7 collective-permute-start.7
  1289.5 92.0 %collective-permute-done.7 = bf16[512,4096]{0,1:T(8,128)(2,1)S(1)} collective-permute-done((bf16[512,4096]{0,1:T(8,128)(2,1)S(1)}, bf16[512,4096]{0,1:T(8,128)(2,1)S(1)}, u32[]{:S(2)}, u32[]{:S(2)}) %collective-permute-start.7) | collective-permute-done | bytes 4194336 | tf_op jit(solution)/shard_map/ppermute | solution.py:14
  1381.5 3.2 broadcast_select_fusion.15
  1384.6 552.1 %collective-permute-done.11 = bf16[8192,1024]{1,0:T(8,128)(2,1)} collective-permute-done((bf16[8192,1024]{1,0:T(8,128)(2,1)}, bf16[8192,1024]{1,0:T(8,128)(2,1)}, u32[]{:S(2)}, u32[]{:S(2)}) %collective-permute-start.11) | collective-permute-done | bytes 16777248 | tf_op jit(solution)/shard_map/ppermute | solution.py:14
  1936.7 25.6 %broadcast_select_fusion.1 = (bf16[8192,1024]{1,0:T(8,128)(2,1)}, bf16[8192,1024]{1,0:T(8,128)(2,1)}) fusion(bf16[8192,1024]{1,0:T(8,128)(2,1)} %collective-permute-done.11, pred[]{:T(512)S(6)} %eq.39, bf16[8192,512]{1,0:T(8,128)(2,1)} %copy-done.5, bf16[8192,512]{1,0:T(8,128)(2,1)} %copy-done.4), kind=kLoop, calls=%fused_computation.13 | loop fusion | flops 50331648 | bytes 67108864 | tf_op jit(solution)/shard_map/jit(_where)/select_n | solution.py:22
  1962.3 27.4 %fusion.26 = bf16[512,2048]{1,0:T(8,128)(2,1)S(1)} fusion(bf16[8192,1024]{1,0:T(8,128)(2,1)} %get-tuple-element.8, bf16[8192,1024]{1,0:T(8,128)(2,1)} %get-tuple-element.7, bf16[512,4096]{0,1:T(8,128)(2,1)} %get-tuple-element.18, bf16[512,4096]{0,1:T(8,128)(2,1)S(1)} %get-tuple-element.17), kind=kOutput, calls=%fused_computation.63 | convolution fusion | flops 17264803840 | bytes 44040192 | tf_op jit(solution)/shard_map/dot_general | solution.py:142
  1989.9 2.6 collective-permute-done.12
  1993.0 0.9 collective-permute-start.13
  1993.9 24.4 %collective-permute-done.13 = bf16[1,2,128,2048]{3,2,1,0:T(8,128)(2,1)S(1)} collective-permute-done((bf16[1,2,128,2048]{3,2,1,0:T(8,128)(2,1)S(1)}, bf16[1,2,128,2048]{3,2,1,0:T(8,128)(2,1)S(1)}, u32[]{:S(2)}, u32[]{:S(2)}) %collective-permute-start.13) | collective-permute-done | bytes 1048608 | tf_op jit(solution)/shard_map/ppermute | solution.py:14
  2018.7 2.8 reshape_reshape.19
  2021.5 4.3 copy.92
  2025.8 2.8 reshape.266
  (58 shorter events, 2.1 us)
Async XLA Ops:
  0.0 362.0 %copy-start = (s32[4,512]{1,0:T(4,128)S(1)}, s32[4,512]{1,0:T(4,128)}, u32[]{:S(2)}) copy-start(s32[4,512]{1,0:T(4,128)} %param.14) | copy-start | bytes 24580
  0.0 254.2 %collective-permute-start.4 = (bf16[2048,2048]{1,0:T(8,128)(2,1)}, bf16[2048,2048]{1,0:T(8,128)(2,1)}, u32[]{:S(2)}, u32[]{:S(2)}) collective-permute-start(bf16[2048,2048]{1,0:T(8,128)(2,1)} %param.10), channel_id=1, source_target_pairs={{0,4},{1,5},{2,6},{3,7},{4,0},{5,1},{6,2},{7,3},{8,12},{9,13},{10,... | collective-permute-start | bytes 25165832 | tf_op jit(solution)/shard_map/ppermute | solution.py:14
  31.8 6.7 copy-start.6
  31.8 200.5 %collective-permute-start.8 = (bf16[2,1,2048,512]{3,2,0,1:T(8,128)(2,1)}, bf16[2,1,2048,512]{3,2,0,1:T(8,128)(2,1)}, u32[]{:S(2)}, u32[]{:S(2)}) collective-permute-start(bf16[2,1,2048,512]{3,2,0,1:T(8,128)(2,1)} %select_bitcast_fusion.1), channel_id=1, source_target_pairs={{0,1},{1,0},{2,3},{3,2},{4,5},{5,4},{6,7},{7,6},{8,9},{9,8},{10,11... | collective-permute-start | bytes 12582920 | tf_op jit(solution)/shard_map/ppermute | solution.py:14
  33.5 5.6 copy-start.13
  38.5 190.2 %collective-permute-start = (bf16[2,2048,256]{1,2,0:T(8,128)(2,1)}, bf16[2,2048,256]{1,2,0:T(8,128)(2,1)}, u32[]{:S(2)}, u32[]{:S(2)}) collective-permute-start(bf16[2,2048,256]{1,2,0:T(8,128)(2,1)} %pad_maximum_fusion.11), channel_id=1, source_target_pairs={{0,4},{1,5},{2,6},{3,7},{4,0},{5,1},{6,2},{7,3},{8,12},{9,13},{10,... | collective-permute-start | bytes 6291464 | tf_op jit(solution)/shard_map/ppermute | solution.py:14
  41.0 236.3 %collective-permute-start.2 = (bf16[128,8192]{1,0:T(8,128)(2,1)}, bf16[128,8192]{1,0:T(8,128)(2,1)}, u32[]{:S(2)}, u32[]{:S(2)}) collective-permute-start(bf16[128,8192]{1,0:T(8,128)(2,1)} %fusion.20), channel_id=1, source_target_pairs={{0,1},{1,0},{2,3},{3,2},{4,5},{5,4},{6,7},{7,6},{8,9},{9,8},{10,11... | collective-permute-start | bytes 6291464 | tf_op jit(solution)/shard_map/ppermute | solution.py:14
  232.4 42.0 %copy-start.10 = (bf16[2,2048,256]{1,2,0:T(8,128)(2,1)}, bf16[2,2048,256]{1,2,0:T(8,128)(2,1)S(1)}, u32[]{:S(2)}) copy-start(bf16[2,2048,256]{1,2,0:T(8,128)(2,1)S(1)} %get-tuple-element.27) | copy-start | bytes 6291460
  252.4 91.8 %collective-permute-start.9 = (bf16[1,2,2048,512]{3,2,1,0:T(8,128)(2,1)S(1)}, bf16[1,2,2048,512]{3,2,1,0:T(8,128)(2,1)S(1)}, u32[]{:S(2)}, u32[]{:S(2)}) collective-permute-start(bf16[1,2,2048,512]{3,2,1,0:T(8,128)(2,1)S(1)} %select_bitcast_fusion), channel_id=1, source_target_pairs={{0,2},{1,3},{2,0},{3,1},{4,6},{5,7},{6,4},{7,5},{8,10},{9,11},{10,... | collective-permute-start | bytes 12582920 | tf_op jit(solution)/shard_map/ppermute | solution.py:14
  260.7 8.6 copy-start.2
  260.7 11.1 copy-start.3
  260.7 13.7 copy-start.11
  271.8 943.1 %collective-permute-start.5 = (bf16[4096,2048]{1,0:T(8,128)(2,1)}, bf16[4096,2048]{1,0:T(8,128)(2,1)}, u32[]{:S(2)}, u32[]{:S(2)}) collective-permute-start(bf16[4096,2048]{1,0:T(8,128)(2,1)} %pad_maximum_fusion), channel_id=1, source_target_pairs={{0,8},{1,9},{2,10},{3,11},{4,12},{5,13},{6,14},{7,15},{8,0},{9,1},... | collective-permute-start | bytes 50331656 | tf_op jit(solution)/shard_map/ppermute | solution.py:14
  274.4 69.9 %slice-start = ((s8[8388608]{0:T(1024)(128)(4,1)}), s8[4194304]{0:T(1024)(128)(4,1)S(1)}, s32[]{:S(2)}) async-start(s8[8388608]{0:T(1024)(128)(4,1)} %bitcast.145), calls=%async_computation | async-start | bytes 8388608
  276.9 67.3 %slice-start.1 = ((s8[8388608]{0:T(1024)(128)(4,1)}), s8[4194304]{0:T(1024)(128)(4,1)S(1)}, s32[]{:S(2)}) async-start(s8[8388608]{0:T(1024)(128)(4,1)} %bitcast.145), calls=%async_computation.1 | async-start | bytes 8388608
  276.9 896.2 %collective-permute-start.1 = (bf16[2,4096,256]{1,2,0:T(8,128)(2,1)}, bf16[2,4096,256]{1,2,0:T(8,128)(2,1)}, u32[]{:S(2)}, u32[]{:S(2)}) collective-permute-start(bf16[2,4096,256]{1,2,0:T(8,128)(2,1)} %pad_maximum_fusion.6), channel_id=1, source_target_pairs={{0,8},{1,9},{2,10},{3,11},{4,12},{5,13},{6,14},{7,15},{8,0},{9,1},... | collective-permute-start | bytes 12582920 | tf_op jit(solution)/shard_map/ppermute | solution.py:14
  281.8 75.2 %copy-start.7 = (bf16[128,8192]{1,0:T(8,128)(2,1)}, bf16[128,8192]{1,0:T(8,128)(2,1)S(1)}, u32[]{:S(2)}) copy-start(bf16[128,8192]{1,0:T(8,128)(2,1)S(1)} %get-tuple-element.29) | copy-start | bytes 6291460
  347.9 9.0 copy-start.9
  355.5 842.0 %collective-permute-start.10 = (bf16[8192,512]{1,0:T(8,128)(2,1)}, bf16[8192,512]{1,0:T(8,128)(2,1)}, u32[]{:S(2)}, u32[]{:S(2)}) collective-permute-start(bf16[8192,512]{1,0:T(8,128)(2,1)} %bitcast.148), channel_id=1, source_target_pairs={{0,4},{1,5},{2,6},{3,7},{4,0},{5,1},{6,2},{7,3},{8,12},{9,13},{10,... | collective-permute-start | bytes 25165832 | tf_op jit(solution)/shard_map/ppermute | solution.py:14
  357.0 3.8 copy-start.14
  359.2 820.5 %collective-permute-start.3 = (bf16[256,8192]{1,0:T(8,128)(2,1)}, bf16[256,8192]{1,0:T(8,128)(2,1)}, u32[]{:S(2)}, u32[]{:S(2)}) collective-permute-start(bf16[256,8192]{1,0:T(8,128)(2,1)} %pad_maximum_fusion.7), channel_id=1, source_target_pairs={{0,2},{1,3},{2,0},{3,1},{4,6},{5,7},{6,4},{7,5},{8,10},{9,11},{10,... | collective-permute-start | bytes 12582920 | tf_op jit(solution)/shard_map/ppermute | solution.py:14
  363.3 816.4 %copy-start.8 = (bf16[128,8192]{1,0:T(8,128)(2,1)S(1)}, bf16[128,8192]{1,0:T(8,128)(2,1)}, u32[]{:S(2)}) copy-start(bf16[128,8192]{1,0:T(8,128)(2,1)} %copy-done.7) | copy-start | bytes 6291460
  1204.0 10.1 copy-start.4
  1204.0 10.9 copy-start.5
  1214.9 721.8 %collective-permute-start.11 = (bf16[8192,1024]{1,0:T(8,128)(2,1)}, bf16[8192,1024]{1,0:T(8,128)(2,1)}, u32[]{:S(2)}, u32[]{:S(2)}) collective-permute-start(bf16[8192,1024]{1,0:T(8,128)(2,1)} %pad_maximum_fusion.1), channel_id=1, source_target_pairs={{0,8},{1,9},{2,10},{3,11},{4,12},{5,13},{6,14},{7,15},{8,0},{9,1},... | collective-permute-start | bytes 50331656 | tf_op jit(solution)/shard_map/ppermute | solution.py:14
  1273.7 6.2 copy-start.12
  1283.9 4.2 collective-permute-start.6
  1288.8 92.7 %collective-permute-start.7 = (bf16[512,4096]{0,1:T(8,128)(2,1)S(1)}, bf16[512,4096]{0,1:T(8,128)(2,1)S(1)}, u32[]{:S(2)}, u32[]{:S(2)}) collective-permute-start(bf16[512,4096]{0,1:T(8,128)(2,1)S(1)} %pad_maximum_fusion.8), channel_id=1, source_target_pairs={{0,2},{1,3},{2,0},{3,1},{4,6},{5,7},{6,4},{7,5},{8,10},{9,11},{10,... | collective-permute-start | bytes 12582920 | tf_op jit(solution)/shard_map/ppermute | solution.py:14
  1989.8 2.7 collective-permute-start.12
  1993.0 25.3 %collective-permute-start.13 = (bf16[1,2,128,2048]{3,2,1,0:T(8,128)(2,1)S(1)}, bf16[1,2,128,2048]{3,2,1,0:T(8,128)(2,1)S(1)}, u32[]{:S(2)}, u32[]{:S(2)}) collective-permute-start(bf16[1,2,128,2048]{3,2,1,0:T(8,128)(2,1)S(1)} %fusion.45), channel_id=1, source_target_pairs={{0,2},{1,3},{2,0},{3,1},{4,6},{5,7},{6,4},{7,5},{8,10},{9,11},{10,... | collective-permute-start | bytes 3145736 | tf_op jit(solution)/shard_map/ppermute | solution.py:14
  2018.7 9.8 copy-start.1
where the time goes:
time: 2040 us; the launch traced here: 2030 us
  waiting for transfers between devices  1730 us (85%)
  other arithmetic  156 us (8%)
  matrix products  72.9 us (4%)
  local copies, waits for them, and re-layouts  51.1 us (3%)
    ppermute x14, waiting for transfers between devices, partner_2(): return lax.ppermute(value, axis, pairs)  1730 us
    select_n x10, other arithmetic, joined(): lower = jnp.where(partner_first, partner, current)  87.3 us
  transfers between devices with their start and end apart: 14, of which 8 were waited for; matrix products, arithmetic and copies ran while one was open for 10% of the time, Pallas kernels for 0%

commit v1 on v0

--- a/solution.py
+++ b/solution.py
@@ -55,7 +55,7 @@
     )
 
 
-def shards(
+def gathered_weight_shards(
     tokens,
     norm_gain,
     query_tiles,
@@ -154,9 +154,145 @@
     return incoming.reshape(owned, PART_TIMELINES * query_head_groups * narrow)
 
 
+def hop(value, pairs):
+    mp = lax.axis_size("mp")
+    span = mp // PART_TIMELINES
+    full = [(a * span + s, b * span + s) for a, b in pairs for s in range(span)]
+    return lax.ppermute(value, "mp", full)
+
+
+def rotated(value, cosine, sine):
+    half = HEAD_SIZE // 2
+    first, second = value[..., :half], value[..., half:]
+    return jnp.concatenate(
+        [first * cosine - second * sine, second * cosine + first * sine], axis=-1
+    )
+
+
+def attention(queries, keys, values, allowed):
+    scores = jnp.einsum("qgd,kd->gqk", queries, keys, preferred_element_type=jnp.float32)
+    raw = jnp.where(allowed, jnp.exp(scores), 0.0)
+    probs = (raw / jnp.sum(raw, axis=-1, keepdims=True)).astype(jnp.bfloat16)
+    heads = jnp.einsum("gqk,kd->qgd", probs, values, preferred_element_type=jnp.float32)
+    return heads.astype(jnp.bfloat16).reshape(queries.shape[0], -1)
+
+
+PIECES = 2
+
+
+def resident_weight_shards(
+    tokens,
+    norm_gain,
+    query_tiles,
+    key_weight_tiles,
+    value_weight_tiles,
+    output_tiles,
+    visits,
+    lengths,
+):
+    ring = PART_TIMELINES
+    device_index = lax.axis_index("mp")
+    plane = device_index // 4
+    place = device_index % 4
+    owned, width = tokens.shape
+    depth = width // ring
+    rows = 4 * owned
+    widened = tokens.astype(jnp.float32)
+    normed = (
+        widened * lax.rsqrt(jnp.mean(widened * widened, axis=1, keepdims=True) + 1e-05) * norm_gain
+    ).astype(jnp.bfloat16)
+
+    slots = []
+    for r in range(ring):
+        start = (plane + r) % ring * depth
+        block = lax.dynamic_slice_in_dim(normed, start, depth, 1)
+        if r > 0:
+            block = hop(block, [(z, (z + r) % ring) for z in range(ring)])
+        pair = jnp.stack([block, partner_2(block, "mp", 1)])
+        other = partner_2(pair, "mp", 0)
+        slots.append(jnp.stack([pair[0], other[0], pair[1], other[1]]).reshape(rows, depth))
+
+    order = [place ^ j for j in range(4)]
+    positions = jnp.concatenate(
+        [o * owned + jnp.arange(owned, dtype=jnp.int32) for o in order]
+    )
+    visit_row = lax.dynamic_index_in_dim(visits, plane, 0, keepdims=False)
+    visit_row = jnp.concatenate(
+        [lax.dynamic_slice_in_dim(visit_row, o * owned, owned, 0) for o in order]
+    )
+    real_count = lax.dynamic_index_in_dim(lengths, plane, 0, keepdims=False)
+    allowed = (visit_row[None, :] <= visit_row[:, None]) & (positions[None, :] < real_count)
+    half = HEAD_SIZE // 2
+    inverse = jnp.power(500000.0, -jnp.arange(half, dtype=jnp.float32) * 2.0 / HEAD_SIZE)
+    angles = positions.astype(jnp.float32)[:, None] * inverse[None, :]
+    cosine, sine = jnp.cos(angles), jnp.sin(angles)
+
+    local_kv = key_weight_tiles.shape[1] // HEAD_SIZE
+    columns = query_tiles.shape[1]
+    repeats = PIECES // local_kv
+    step = columns // PIECES
+    right = [(z, z + 1) for z in range(ring - 1)]
+    left = [(z + 1, z) for z in range(ring - 1)]
+    totals = [None] * ring
+    keys = values = None
+    for piece in range(PIECES):
+        has_kv = piece % repeats == 0
+        weight = query_tiles[:, piece * step : (piece + 1) * step]
+        if has_kv:
+            kv = piece // repeats
+            span = slice(kv * HEAD_SIZE, (kv + 1) * HEAD_SIZE)
+            weight = jnp.concatenate(
+                [weight, key_weight_tiles[:, span], value_weight_tiles[:, span]], axis=1
+            )
+
+        def part(r):
+            return jnp.dot(slots[r], weight, preferred_element_type=jnp.float32)
+
+        going_right, going_left = part(1), part(3)
+        middle = None
+        for k in range(1, ring):
+            arrived_right = hop(going_right.astype(jnp.bfloat16), right[:k])
+            arrived_left = hop(going_left.astype(jnp.bfloat16), left[ring - 1 - k :])
+            if k < ring - 1:
+                going_right = part(k + 1) + arrived_right.astype(jnp.float32)
+                going_left = part(ring - 1 - k) + arrived_left.astype(jnp.float32)
+        summed = part(0) + arrived_right.astype(jnp.float32) + arrived_left.astype(jnp.float32)
+        if has_kv:
+            keys = rotated(summed[:, step : step + HEAD_SIZE], cosine, sine).astype(jnp.bfloat16)
+            values = summed[:, step + HEAD_SIZE :].astype(jnp.bfloat16)
+        queries = rotated(
+            summed[:, :step].reshape(rows, -1, HEAD_SIZE), cosine[:, None], sine[:, None]
+        )
+        queries = (queries * HEAD_SIZE ** (-0.5)).astype(jnp.bfloat16)
+        own = attention(queries, keys, values, allowed)
+        from_left, from_right = [own], [own]
+        for k in range(1, ring):
+            from_left.append(hop(from_left[-1], right[k - 1 :]))
+            from_right.append(hop(from_right[-1], left[: ring - k]))
+        out_rows = output_tiles[piece * step : (piece + 1) * step]
+        for r in range(ring):
+            block = own if r == 0 else jnp.where(plane >= r, from_left[r], from_right[ring - r])
+            product = jnp.dot(block, out_rows, preferred_element_type=jnp.float32)
+            totals[r] = product if totals[r] is None else totals[r] + product
+
+    out = jnp.zeros((owned, width), jnp.bfloat16)
+    for r in (0, 2, 3, 1):
+        four = totals[r].reshape(4, owned, depth)
+        away = jnp.stack([four[1], four[3]]).astype(jnp.bfloat16)
+        arrived = partner_2(away, "mp", 0).astype(jnp.float32)
+        far = (four[2] + arrived[1]).astype(jnp.bfloat16)
+        near = four[0] + arrived[0] + partner_2(far, "mp", 1).astype(jnp.float32)
+        block = near.astype(jnp.bfloat16)
+        if r > 0:
+            block = hop(block, [(z, (z - r) % ring) for z in range(ring)])
+        out = lax.dynamic_update_slice_in_dim(out, block, (plane + r) % ring * depth, 1)
+    return out
+
+
 def solution(mesh):
+    resident = mesh.shape["mp"] == 4 * PART_TIMELINES
     return jax.shard_map(
-        shards,
+        resident_weight_shards if resident else gathered_weight_shards,
         mesh=mesh,
         in_specs=(
             P(("group", "mp"), None),

time: 2040 us -> 579 us (0.28)
  waiting for transfers between devices: 1730 us -> 296 us
  starting transfers between devices: 12.7 us -> 161 us
  other arithmetic: 156 us -> 20.5 us
  local copies, waits for them, and re-layouts: 51.1 us -> 17.7 us
    ppermute x14 -> x16, waiting for transfers between devices: 1730 us -> 37.7 us  [partner_2(): return lax.ppermute(value, axis, pairs)]
    ppermute x0 -> x30, waiting for transfers between devices: none -> 258 us  [hop(): return lax.ppermute(value, 'mp', full)]
    ppermute x0 -> x30, starting transfers between devices: none -> 150 us  [hop(): return lax.ppermute(value, 'mp', full)]
    select_n x14 -> x0, other arithmetic: 96.3 us -> none  [the longest x10 87.3 us: joined(): lower = jnp.where(partner_first, partner, current)]
    another operation x10 -> x13, other arithmetic: 31.2 us -> 8.23 us  [the longest x4 2.4 us: resident_weight_shards(): pair = jnp.stack([block, partner_2(block, 'mp', 1)])]
    concatenate x5 -> x1, other arithmetic: 22.9 us -> 0.01 us  [resident_weight_shards(): jnp.concatenate([lax.dynamic_slice_in_dim(visit_row, o * owned, owned, 0)...]
    dot_general x5 -> x20, matrix products: 72.9 us -> 72.8 us  [the longest x8 34 us: part(): return jnp.dot(slots[r], weight, preferred_element_type=jnp.float32)]
  transfers between devices with their start and end apart: 14 -> 46, of which waited for: 8 -> 19; matrix products, arithmetic and copies ran while one was open for 10% -> 15% of each run, Pallas kernels for 0% -> 0%
where the time goes in v1:
time: 579 us; the launch traced here: 570 us
  waiting for transfers between devices  296 us (51%)
  starting transfers between devices  161 us (28%)
  matrix products  72.8 us (13%)
  other arithmetic  20.5 us (4%)
  local copies, waits for them, and re-layouts  17.7 us (3%)
    ppermute x30, waiting for transfers between devices, hop(): return lax.ppermute(value, 'mp', full)  258 us
    ppermute x30, starting transfers between devices, hop(): return lax.ppermute(value, 'mp', full)  150 us
    ppermute x16, waiting for transfers between devices, partner_2(): return lax.ppermute(value, axis, pairs)  37.7 us
    dot_general x8, matrix products, part(): return jnp.dot(slots[r], weight, preferred_element_type=jnp.float32)  34 us
    dot_general x8, matrix products, resident_weight_shards(): product = jnp.dot(block, out_rows, preferred_element_type=jnp.float32)  28.4 us
  transfers between devices with their start and end apart: 46, of which 19 were waited for; matrix products, arithmetic and copies ran while one was open for 15% of the time, Pallas kernels for 0%

profile of v1, /device:TPU:0, one launch (start us, length us, event | category | flops | bytes accessed | tf_op | source)
XLA Modules:
  0.0 569.8 jit_solution(7985719676235537235)
XLA Ops:
  0.0 2.2 fusion.2
  2.3 1.5 fusion.4
  4.0 3.1 collective-permute-start.8
  7.1 2.6 collective-permute-start.5
  11.1 1.5 collective-permute-start
  12.6 9.5 %collective-permute-done.8 = bf16[128,2048]{1,0:T(8,128)(2,1)S(1)} collective-permute-done((bf16[128,2048]{1,0:T(8,128)(2,1)S(1)}, bf16[128,2048]{1,0:T(8,128)(2,1)S(1)}, u32[]{:S(2)}, u32[]{:S(2)}) %collective-permute-start.8) | collective-permute-done | bytes 524320 | tf_op jit(solution)/shard_map/ppermute | solution.py:161
  22.0 1.8 collective-permute-start.9
  23.8 3.8 fusion.103
  27.6 16.1 %collective-permute-done.5 = bf16[128,2048]{1,0:T(8,128)(2,1)S(1)} collective-permute-done((bf16[128,2048]{1,0:T(8,128)(2,1)S(1)}, bf16[128,2048]{1,0:T(8,128)(2,1)S(1)}, u32[]{:S(2)}, u32[]{:S(2)}) %collective-permute-start.5) | collective-permute-done | bytes 524320 | tf_op jit(solution)/shard_map/ppermute | solution.py:161
  47.6 1.6 fusion.106
  49.1 9.3 %collective-permute-done.6 = bf16[128,2048]{1,0:T(8,128)(2,1)S(1)} collective-permute-done((bf16[128,2048]{1,0:T(8,128)(2,1)S(1)}, bf16[128,2048]{1,0:T(8,128)(2,1)S(1)}, u32[]{:S(2)}, u32[]{:S(2)}) %collective-permute-start.6) | collective-permute-done | bytes 524320 | tf_op jit(solution)/shard_map/ppermute | solution.py:14
  58.7 10.0 %collective-permute-done.3 = bf16[128,2048]{1,0:T(8,128)(2,1)S(1)} collective-permute-done((bf16[128,2048]{1,0:T(8,128)(2,1)S(1)}, bf16[128,2048]{1,0:T(8,128)(2,1)S(1)}, u32[]{:S(2)}, u32[]{:S(2)}) %collective-permute-start.3) | collective-permute-done | bytes 524320 | tf_op jit(solution)/shard_map/ppermute | solution.py:14
  70.6 1.9 copy-done.5
  72.5 4.4 fusion.112
  76.9 10.9 %collective-permute-start.11 = (bf16[512,1280]{1,0:T(8,128)(2,1)S(1)}, bf16[512,1280]{1,0:T(8,128)(2,1)S(1)}, u32[]{:S(2)}, u32[]{:S(2)}) collective-permute-start(bf16[512,1280]{1,0:T(8,128)(2,1)S(1)} %get-tuple-element.59), channel_id=1, source_target_pairs={{0,4},{1,5},{2,6},{3,7},{16,20},{17,21},{18,22},{19,23}} | collective-permute-start | bytes 3932168 | tf_op jit(solution)/shard_map/ppermute | solution.py:161
  87.9 2.9 fusion.113
  92.6 24.2 %collective-permute-done.11 = bf16[512,1280]{1,0:T(8,128)(2,1)S(1)} collective-permute-done((bf16[512,1280]{1,0:T(8,128)(2,1)S(1)}, bf16[512,1280]{1,0:T(8,128)(2,1)S(1)}, u32[]{:S(2)}, u32[]{:S(2)}) %collective-permute-start.11) | collective-permute-done | bytes 1310752 | tf_op jit(solution)/shard_map/ppermute | solution.py:161
  116.8 4.4 add_convert_fusion.7
  121.2 4.7 collective-permute-start.12
  126.3 18.6 %collective-permute-done.17 = bf16[512,1280]{1,0:T(8,128)(2,1)S(1)} collective-permute-done((bf16[512,1280]{1,0:T(8,128)(2,1)S(1)}, bf16[512,1280]{1,0:T(8,128)(2,1)S(1)}, u32[]{:S(2)}, u32[]{:S(2)}) %collective-permute-start.17) | collective-permute-done | bytes 1310752 | tf_op jit(solution)/shard_map/ppermute | solution.py:161
  144.9 4.8 add_convert_fusion.3
  149.7 5.5 collective-permute-start.18
  155.2 17.8 %collective-permute-done.12 = bf16[512,1280]{1,0:T(8,128)(2,1)S(1)} collective-permute-done((bf16[512,1280]{1,0:T(8,128)(2,1)S(1)}, bf16[512,1280]{1,0:T(8,128)(2,1)S(1)}, u32[]{:S(2)}, u32[]{:S(2)}) %collective-permute-start.12) | collective-permute-done | bytes 1310752 | tf_op jit(solution)/shard_map/ppermute | solution.py:161
  173.0 5.1 add_convert_fusion.6
  178.1 1.7 collective-permute-start.14
  181.4 19.4 %collective-permute-done.18 = bf16[512,1280]{1,0:T(8,128)(2,1)} collective-permute-done((bf16[512,1280]{1,0:T(8,128)(2,1)}, bf16[512,1280]{1,0:T(8,128)(2,1)}, u32[]{:S(2)}, u32[]{:S(2)}) %collective-permute-start.18) | collective-permute-done | bytes 1310752 | tf_op jit(solution)/shard_map/ppermute | solution.py:161
  200.8 6.4 %add_convert_fusion.2 = (bf16[512,1280]{1,0:T(8,128)(2,1)S(1)}, bf16[512,1280]{1,0:T(8,128)(2,1)S(1)}) fusion(bf16[512,1280]{1,0:T(8,128)(2,1)} %collective-permute-done.18, bf16[512,2048]{1,0:T(8,128)(2,1)} %bitcast.158, bf16[2048,128]{1,0:T(8,128)(2,1)} %get-tuple-element.77, bf16[2048,128]{1,0:T(8,128)(2,1)} %get-tuple-element.37, ...), kind=kOutput, calls=%fused_computation.37 | convolution fusion | flops 2702704640 | bytes 11272192 | tf_op jit(solution)/shard_map/dot_general | solution.py:249
  208.0 1.8 add_convert_fusion.5
  212.7 5.0 collective-permute-start.13
  222.5 28.9 %collective-permute-start.19 = (bf16[512,1280]{1,0:T(8,128)(2,1)S(1)}, bf16[512,1280]{1,0:T(8,128)(2,1)S(1)}, u32[]{:S(2)}, u32[]{:S(2)}) collective-permute-start(bf16[512,1280]{1,0:T(8,128)(2,1)S(1)} %get-tuple-element.17), channel_id=1, source_target_pairs={{0,4},{1,5},{2,6},{3,7},{4,8},{5,9},{6,10},{7,11},{8,12},{9,13},{1... | collective-permute-start | bytes 3932168 | tf_op jit(solution)/shard_map/ppermute | solution.py:161
  251.8 2.0 collective-permute-start.22
  253.8 20.7 %collective-permute-done.16 = bf16[512,1280]{1,0:T(8,128)(2,1)S(1)} collective-permute-done((bf16[512,1280]{1,0:T(8,128)(2,1)S(1)}, bf16[512,1280]{1,0:T(8,128)(2,1)S(1)}, u32[]{:S(2)}, u32[]{:S(2)}) %collective-permute-start.16) | collective-permute-done | bytes 1310752 | tf_op jit(solution)/shard_map/ppermute | solution.py:161
  274.5 2.9 fusion.8
  278.9 23.9 %collective-permute-done.22 = bf16[512,1280]{1,0:T(8,128)(2,1)S(1)} collective-permute-done((bf16[512,1280]{1,0:T(8,128)(2,1)S(1)}, bf16[512,1280]{1,0:T(8,128)(2,1)S(1)}, u32[]{:S(2)}, u32[]{:S(2)}) %collective-permute-start.22) | collective-permute-done | bytes 1310752 | tf_op jit(solution)/shard_map/ppermute | solution.py:161
  302.9 2.9 fusion.7
  311.6 3.6 fusion.1
  315.2 3.3 fusion.23
  318.5 1.6 collective-permute-start.31
  320.0 29.5 %collective-permute-start.29 = (bf16[512,1024]{0,1:T(8,128)(2,1)S(1)}, bf16[512,1024]{0,1:T(8,128)(2,1)}, u32[]{:S(2)}, u32[]{:S(2)}) collective-permute-start(bf16[512,1024]{0,1:T(8,128)(2,1)S(1)} %bitcast.178), channel_id=1, source_target_pairs={{0,4},{1,5},{2,6},{3,7},{4,8},{5,9},{6,10},{7,11},{8,12},{9,13},{1... | collective-permute-start | bytes 3145736 | tf_op jit(solution)/shard_map/ppermute | solution.py:161
  349.5 2.1 fusion.24
  352.9 7.7 %collective-permute-start.25 = (bf16[512,1024]{0,1:T(8,128)(2,1)S(1)}, bf16[512,1024]{0,1:T(8,128)(2,1)S(1)}, u32[]{:S(2)}, u32[]{:S(2)}) collective-permute-start(bf16[512,1024]{0,1:T(8,128)(2,1)S(1)} %bitcast.181), channel_id=1, source_target_pairs={{0,4},{1,5},{2,6},{3,7},{4,8},{5,9},{6,10},{7,11},{8,12},{9,13},{1... | collective-permute-start | bytes 3145736 | tf_op jit(solution)/shard_map/ppermute | solution.py:161
  360.7 2.5 fusion.19
  363.2 4.6 fusion.114
  369.0 1.8 collective-permute-done.31
  372.0 21.1 %collective-permute-done.27 = bf16[512,1024]{0,1:T(8,128)(2,1)S(1)} collective-permute-done((bf16[512,1024]{0,1:T(8,128)(2,1)S(1)}, bf16[512,1024]{0,1:T(8,128)(2,1)S(1)}, u32[]{:S(2)}, u32[]{:S(2)}) %collective-permute-start.27) | collective-permute-done | bytes 1048608 | tf_op jit(solution)/shard_map/ppermute | solution.py:161
  394.4 1.7 collective-permute-start.30
  398.4 17.3 %collective-permute-done.32 = bf16[512,1024]{0,1:T(8,128)(2,1)} collective-permute-done((bf16[512,1024]{0,1:T(8,128)(2,1)}, bf16[512,1024]{0,1:T(8,128)(2,1)}, u32[]{:S(2)}, u32[]{:S(2)}) %collective-permute-start.32) | collective-permute-done | bytes 1048608 | tf_op jit(solution)/shard_map/ppermute | solution.py:161
  417.0 21.2 %collective-permute-done.28 = bf16[512,1024]{0,1:T(8,128)(2,1)} collective-permute-done((bf16[512,1024]{0,1:T(8,128)(2,1)S(1)}, bf16[512,1024]{0,1:T(8,128)(2,1)}, u32[]{:S(2)}, u32[]{:S(2)}) %collective-permute-start.28) | collective-permute-done | bytes 1048608 | tf_op jit(solution)/shard_map/ppermute | solution.py:161
  439.5 5.2 fusion.13
  444.7 5.2 fusion.115
  451.8 1.9 collective-permute-start.36
  453.6 6.9 %collective-permute-done.42 = bf16[512,1024]{0,1:T(8,128)(2,1)S(1)} collective-permute-done((bf16[512,1024]{0,1:T(8,128)(2,1)}, bf16[512,1024]{0,1:T(8,128)(2,1)S(1)}, u32[]{:S(2)}, u32[]{:S(2)}) %collective-permute-start.42) | collective-permute-done | bytes 1048608 | tf_op jit(solution)/shard_map/ppermute | solution.py:161
  460.5 2.4 fusion.9
  463.0 18.1 %collective-permute-done.41 = bf16[512,1024]{0,1:T(8,128)(2,1)S(1)} collective-permute-done((bf16[512,1024]{0,1:T(8,128)(2,1)}, bf16[512,1024]{0,1:T(8,128)(2,1)S(1)}, u32[]{:S(2)}, u32[]{:S(2)}) %collective-permute-start.41) | collective-permute-done | bytes 1048608 | tf_op jit(solution)/shard_map/ppermute | solution.py:161
  481.1 2.5 fusion.117
  483.8 3.7 fusion.11
  487.5 2.5 fusion.116
  491.1 1.6 collective-permute-start.34
  495.3 10.7 %collective-permute-done.34 = bf16[128,2048]{1,0:T(8,128)(2,1)S(1)} collective-permute-done((bf16[128,2048]{1,0:T(8,128)(2,1)S(1)}, bf16[128,2048]{1,0:T(8,128)(2,1)S(1)}, u32[]{:S(2)}, u32[]{:S(2)}) %collective-permute-start.34) | collective-permute-done | bytes 524320 | tf_op jit(solution)/shard_map/ppermute | solution.py:14
  506.1 12.7 %collective-permute-start.35 = (bf16[128,2048]{1,0:T(8,128)(2,1)S(1)}, bf16[128,2048]{1,0:T(8,128)(2,1)S(1)}, u32[]{:S(2)}, u32[]{:S(2)}) collective-permute-start(bf16[128,2048]{1,0:T(8,128)(2,1)S(1)} %fusion.43), channel_id=1, source_target_pairs={{0,8},{1,9},{2,10},{3,11},{4,12},{5,13},{6,14},{7,15},{8,0},{9,1},... | collective-permute-start | bytes 1572872 | tf_op jit(solution)/shard_map/ppermute | solution.py:161
  519.2 1.6 collective-permute-start.39
  520.8 7.7 %collective-permute-done.44 = bf16[128,2048]{1,0:T(8,128)(2,1)S(1)} collective-permute-done((bf16[128,2048]{1,0:T(8,128)(2,1)S(1)}, bf16[128,2048]{1,0:T(8,128)(2,1)S(1)}, u32[]{:S(2)}, u32[]{:S(2)}) %collective-permute-start.44) | collective-permute-done | bytes 524320 | tf_op jit(solution)/shard_map/ppermute | solution.py:14
  528.6 15.9 %collective-permute-start.45 = (bf16[128,2048]{1,0:T(8,128)(2,1)S(1)}, bf16[128,2048]{1,0:T(8,128)(2,1)S(1)}, u32[]{:S(2)}, u32[]{:S(2)}) collective-permute-start(bf16[128,2048]{1,0:T(8,128)(2,1)S(1)} %fusion.33), channel_id=1, source_target_pairs={{0,12},{1,13},{2,14},{3,15},{4,0},{5,1},{6,2},{7,3},{8,4},{9,5},{1... | collective-permute-start | bytes 1572872 | tf_op jit(solution)/shard_map/ppermute | solution.py:161
  545.3 21.9 %collective-permute-done.40 = bf16[128,2048]{1,0:T(8,128)(2,1)S(1)} collective-permute-done((bf16[128,2048]{1,0:T(8,128)(2,1)S(1)}, bf16[128,2048]{1,0:T(8,128)(2,1)S(1)}, u32[]{:S(2)}, u32[]{:S(2)}) %collective-permute-start.40) | collective-permute-done | bytes 524320 | tf_op jit(solution)/shard_map/ppermute | solution.py:161
  (191 shorter events, 46.2 us)
Async XLA Ops:
  2.3 21.5 %copy-start.1 = (bf16[2048,2048]{1,0:T(8,128)(2,1)S(1)}, bf16[2048,2048]{1,0:T(8,128)(2,1)}, u32[]{:S(2)}) copy-start(bf16[2048,2048]{1,0:T(8,128)(2,1)} %param.10) | copy-start | bytes 25165828
  4.0 18.0 %collective-permute-start.8 = (bf16[128,2048]{1,0:T(8,128)(2,1)S(1)}, bf16[128,2048]{1,0:T(8,128)(2,1)S(1)}, u32[]{:S(2)}, u32[]{:S(2)}) collective-permute-start(bf16[128,2048]{1,0:T(8,128)(2,1)S(1)} %get-tuple-element.34), channel_id=1, source_target_pairs={{0,4},{1,5},{2,6},{3,7},{4,8},{5,9},{6,10},{7,11},{8,12},{9,13},{1... | collective-permute-start | bytes 1572872 | tf_op jit(solution)/shard_map/ppermute | solution.py:161
  7.1 36.6 %collective-permute-start.5 = (bf16[128,2048]{1,0:T(8,128)(2,1)S(1)}, bf16[128,2048]{1,0:T(8,128)(2,1)S(1)}, u32[]{:S(2)}, u32[]{:S(2)}) collective-permute-start(bf16[128,2048]{1,0:T(8,128)(2,1)S(1)} %get-tuple-element.35), channel_id=1, source_target_pairs={{0,8},{1,9},{2,10},{3,11},{4,12},{5,13},{6,14},{7,15},{8,0},{9,1},... | collective-permute-start | bytes 1572872 | tf_op jit(solution)/shard_map/ppermute | solution.py:161
  9.7 35.5 %collective-permute-start.2 = (bf16[128,2048]{1,0:T(8,128)(2,1)S(1)}, bf16[128,2048]{1,0:T(8,128)(2,1)S(1)}, u32[]{:S(2)}, u32[]{:S(2)}) collective-permute-start(bf16[128,2048]{1,0:T(8,128)(2,1)S(1)} %get-tuple-element.33), channel_id=1, source_target_pairs={{0,12},{1,13},{2,14},{3,15},{4,0},{5,1},{6,2},{7,3},{8,4},{9,5},{1... | collective-permute-start | bytes 1572872 | tf_op jit(solution)/shard_map/ppermute | solution.py:161
  11.1 200.4 %collective-permute-start = (bf16[128,2048]{1,0:T(8,128)(2,1)S(1)}, bf16[128,2048]{1,0:T(8,128)(2,1)}, u32[]{:S(2)}, u32[]{:S(2)}) collective-permute-start(bf16[128,2048]{1,0:T(8,128)(2,1)S(1)} %get-tuple-element.36), channel_id=1, source_target_pairs={{0,2},{1,3},{2,0},{3,1},{4,6},{5,7},{6,4},{7,5},{8,10},{9,11},{10,... | collective-permute-start | bytes 1572872 | tf_op jit(solution)/shard_map/ppermute | solution.py:14
  22.0 23.7 %collective-permute-start.9 = (bf16[128,2048]{1,0:T(8,128)(2,1)S(1)}, bf16[128,2048]{1,0:T(8,128)(2,1)S(1)}, u32[]{:S(2)}, u32[]{:S(2)}) collective-permute-start(bf16[128,2048]{1,0:T(8,128)(2,1)S(1)} %collective-permute-done.8), channel_id=1, source_target_pairs={{0,2},{1,3},{2,0},{3,1},{4,6},{5,7},{6,4},{7,5},{8,10},{9,11},{10,... | collective-permute-start | bytes 1572872 | tf_op jit(solution)/shard_map/ppermute | solution.py:14
  27.6 20.0 %copy-start.23 = (bf16[2048,256]{1,0:T(8,128)(2,1)S(1)}, bf16[2048,256]{1,0:T(8,128)(2,1)}, u32[]{:S(2)}) copy-start(bf16[2048,256]{1,0:T(8,128)(2,1)} %param.11) | copy-start | bytes 3145732
  27.6 20.0 %copy-start.24 = (bf16[2048,256]{1,0:T(8,128)(2,1)S(1)}, bf16[2048,256]{1,0:T(8,128)(2,1)}, u32[]{:S(2)}) copy-start(bf16[2048,256]{1,0:T(8,128)(2,1)} %param.12) | copy-start | bytes 3145732
  43.7 14.8 %collective-permute-start.6 = (bf16[128,2048]{1,0:T(8,128)(2,1)S(1)}, bf16[128,2048]{1,0:T(8,128)(2,1)S(1)}, u32[]{:S(2)}, u32[]{:S(2)}) collective-permute-start(bf16[128,2048]{1,0:T(8,128)(2,1)S(1)} %collective-permute-done.5), channel_id=1, source_target_pairs={{0,2},{1,3},{2,0},{3,1},{4,6},{5,7},{6,4},{7,5},{8,10},{9,11},{10,... | collective-permute-start | bytes 1572872 | tf_op jit(solution)/shard_map/ppermute | solution.py:14
  45.2 23.5 %copy-start.13 = (bf16[128,2048]{1,0:T(8,128)(2,1)}, bf16[128,2048]{1,0:T(8,128)(2,1)S(1)}, u32[]{:S(2)}) copy-start(bf16[128,2048]{1,0:T(8,128)(2,1)S(1)} %collective-permute-done.2) | copy-start | bytes 1572868
  45.2 23.5 %collective-permute-start.3 = (bf16[128,2048]{1,0:T(8,128)(2,1)S(1)}, bf16[128,2048]{1,0:T(8,128)(2,1)S(1)}, u32[]{:S(2)}, u32[]{:S(2)}) collective-permute-start(bf16[128,2048]{1,0:T(8,128)(2,1)S(1)} %collective-permute-done.2), channel_id=1, source_target_pairs={{0,2},{1,3},{2,0},{3,1},{4,6},{5,7},{6,4},{7,5},{8,10},{9,11},{10,... | collective-permute-start | bytes 1572872 | tf_op jit(solution)/shard_map/ppermute | solution.py:14
  47.6 21.3 %collective-permute-start.10 = (bf16[2,128,2048]{2,1,0:T(8,128)(2,1)}, bf16[2,128,2048]{2,1,0:T(8,128)(2,1)}, u32[]{:S(2)}, u32[]{:S(2)}) collective-permute-start(bf16[2,128,2048]{2,1,0:T(8,128)(2,1)} %pad_maximum_fusion.9), channel_id=1, source_target_pairs={{0,1},{1,0},{2,3},{3,2},{4,5},{5,4},{6,7},{7,6},{8,9},{9,8},{10,11... | collective-permute-start | bytes 3145736 | tf_op jit(solution)/shard_map/ppermute | solution.py:14
  58.6 33.6 %collective-permute-start.7 = (bf16[2,128,2048]{2,1,0:T(8,128)(2,1)S(1)}, bf16[2,128,2048]{2,1,0:T(8,128)(2,1)S(1)}, u32[]{:S(2)}, u32[]{:S(2)}) collective-permute-start(bf16[2,128,2048]{2,1,0:T(8,128)(2,1)S(1)} %pad_maximum_fusion.8), channel_id=1, source_target_pairs={{0,1},{1,0},{2,3},{3,2},{4,5},{5,4},{6,7},{7,6},{8,9},{9,8},{10,11... | collective-permute-start | bytes 3145736 | tf_op jit(solution)/shard_map/ppermute | solution.py:14
  68.8 57.1 %collective-permute-start.4 = (bf16[2,128,2048]{2,1,0:T(8,128)(2,1)S(1)}, bf16[2,128,2048]{2,1,0:T(8,128)(2,1)S(1)}, u32[]{:S(2)}, u32[]{:S(2)}) collective-permute-start(bf16[2,128,2048]{2,1,0:T(8,128)(2,1)S(1)} %pad_maximum_fusion.7), channel_id=1, source_target_pairs={{0,1},{1,0},{2,3},{3,2},{4,5},{5,4},{6,7},{7,6},{8,9},{9,8},{10,11... | collective-permute-start | bytes 3145736 | tf_op jit(solution)/shard_map/ppermute | solution.py:14
  72.5 15.4 %copy-start.25 = (bf16[2048,128]{1,0:T(8,128)(2,1)S(1)}, bf16[2048,128]{1,0:T(8,128)(2,1)}, u32[]{:S(2)}) copy-start(bf16[2048,128]{1,0:T(8,128)(2,1)} %get-tuple-element.37) | copy-start | bytes 1572868
  72.5 15.4 %copy-start.27 = (bf16[2048,128]{1,0:T(8,128)(2,1)S(1)}, bf16[2048,128]{1,0:T(8,128)(2,1)}, u32[]{:S(2)}) copy-start(bf16[2048,128]{1,0:T(8,128)(2,1)} %get-tuple-element.77) | copy-start | bytes 1572868
  76.9 39.9 %collective-permute-start.11 = (bf16[512,1280]{1,0:T(8,128)(2,1)S(1)}, bf16[512,1280]{1,0:T(8,128)(2,1)S(1)}, u32[]{:S(2)}, u32[]{:S(2)}) collective-permute-start(bf16[512,1280]{1,0:T(8,128)(2,1)S(1)} %get-tuple-element.59), channel_id=1, source_target_pairs={{0,4},{1,5},{2,6},{3,7},{16,20},{17,21},{18,22},{19,23}} | collective-permute-start | bytes 3932168 | tf_op jit(solution)/shard_map/ppermute | solution.py:161
  90.8 54.1 %collective-permute-start.17 = (bf16[512,1280]{1,0:T(8,128)(2,1)S(1)}, bf16[512,1280]{1,0:T(8,128)(2,1)S(1)}, u32[]{:S(2)}, u32[]{:S(2)}) collective-permute-start(bf16[512,1280]{1,0:T(8,128)(2,1)S(1)} %get-tuple-element.63), channel_id=1, source_target_pairs={{0,4},{1,5},{2,6},{3,7},{16,20},{17,21},{18,22},{19,23}} | collective-permute-start | bytes 3932168 | tf_op jit(solution)/shard_map/ppermute | solution.py:161
  121.2 51.8 %collective-permute-start.12 = (bf16[512,1280]{1,0:T(8,128)(2,1)S(1)}, bf16[512,1280]{1,0:T(8,128)(2,1)S(1)}, u32[]{:S(2)}, u32[]{:S(2)}) collective-permute-start(bf16[512,1280]{1,0:T(8,128)(2,1)S(1)} %get-tuple-element.61), channel_id=1, source_target_pairs={{0,4},{1,5},{2,6},{3,7},{4,8},{5,9},{6,10},{7,11},{16,20},{17,21},... | collective-permute-start | bytes 3932168 | tf_op jit(solution)/shard_map/ppermute | solution.py:161
  126.3 46.7 %copy-start.12 = (bf16[4,128,2048]{2,1,0:T(8,128)(2,1)}, bf16[4,128,2048]{2,1,0:T(8,128)(2,1)S(1)}, u32[]{:S(2)}) copy-start(bf16[4,128,2048]{2,1,0:T(8,128)(2,1)S(1)} %pad_maximum_fusion.3) | copy-start | bytes 6291460
  149.7 51.0 %collective-permute-start.18 = (bf16[512,1280]{1,0:T(8,128)(2,1)}, bf16[512,1280]{1,0:T(8,128)(2,1)}, u32[]{:S(2)}, u32[]{:S(2)}) collective-permute-start(bf16[512,1280]{1,0:T(8,128)(2,1)} %get-tuple-element.65), channel_id=1, source_target_pairs={{0,4},{1,5},{2,6},{3,7},{4,8},{5,9},{6,10},{7,11},{16,20},{17,21},... | collective-permute-start | bytes 3932168 | tf_op jit(solution)/shard_map/ppermute | solution.py:161
  178.1 29.8 %collective-permute-start.14 = (bf16[512,1280]{1,0:T(8,128)(2,1)}, bf16[512,1280]{1,0:T(8,128)(2,1)}, u32[]{:S(2)}, u32[]{:S(2)}) collective-permute-start(bf16[512,1280]{1,0:T(8,128)(2,1)} %get-tuple-element.20), channel_id=1, source_target_pairs={{12,8},{13,9},{14,10},{15,11},{28,24},{29,25},{30,26},{31,27}} | collective-permute-start | bytes 3932168 | tf_op jit(solution)/shard_map/ppermute | solution.py:161
  181.4 26.6 %copy-start.9 = (f32[512,1280]{1,0:T(8,128)S(1)}, f32[512,1280]{1,0:T(8,128)}, u32[]{:S(2)}) copy-start(f32[512,1280]{1,0:T(8,128)} %get-tuple-element.62) | copy-start | bytes 7864324
  207.2 10.6 %collective-permute-start.20 = (bf16[512,1280]{1,0:T(8,128)(2,1)S(1)}, bf16[512,1280]{1,0:T(8,128)(2,1)S(1)}, u32[]{:S(2)}, u32[]{:S(2)}) collective-permute-start(bf16[512,1280]{1,0:T(8,128)(2,1)S(1)} %get-tuple-element.18), channel_id=1, source_target_pairs={{12,8},{13,9},{14,10},{15,11},{28,24},{29,25},{30,26},{31,27}} | collective-permute-start | bytes 3932168 | tf_op jit(solution)/shard_map/ppermute | solution.py:161
  209.8 9.3 %collective-permute-start.15 = (bf16[512,1280]{1,0:T(8,128)(2,1)S(1)}, bf16[512,1280]{1,0:T(8,128)(2,1)S(1)}, u32[]{:S(2)}, u32[]{:S(2)}) collective-permute-start(bf16[512,1280]{1,0:T(8,128)(2,1)S(1)} %add_convert_fusion.5), channel_id=1, source_target_pairs={{8,4},{9,5},{10,6},{11,7},{12,8},{13,9},{14,10},{15,11},{24,20},{2... | collective-permute-start | bytes 3932168 | tf_op jit(solution)/shard_map/ppermute | solution.py:161
  212.6 8.5 %collective-permute-start.1 = (bf16[2,128,2048]{2,1,0:T(8,128)(2,1)S(1)}, bf16[2,128,2048]{2,1,0:T(8,128)(2,1)S(1)}, u32[]{:S(2)}, u32[]{:S(2)}) collective-permute-start(bf16[2,128,2048]{2,1,0:T(8,128)(2,1)S(1)} %pad_maximum_fusion.6), channel_id=1, source_target_pairs={{0,1},{1,0},{2,3},{3,2},{4,5},{5,4},{6,7},{7,6},{8,9},{9,8},{10,11... | collective-permute-start | bytes 3145736 | tf_op jit(solution)/shard_map/ppermute | solution.py:14
  212.7 41.1 %collective-permute-start.13 = (bf16[512,1280]{1,0:T(8,128)(2,1)S(1)}, bf16[512,1280]{1,0:T(8,128)(2,1)S(1)}, u32[]{:S(2)}, u32[]{:S(2)}) collective-permute-start(bf16[512,1280]{1,0:T(8,128)(2,1)S(1)} %copy-done.33), channel_id=1, source_target_pairs={{0,4},{1,5},{2,6},{3,7},{4,8},{5,9},{6,10},{7,11},{8,12},{9,13},{1... | collective-permute-start | bytes 3932168 | tf_op jit(solution)/shard_map/ppermute | solution.py:161
  218.2 33.3 %collective-permute-start.21 = (bf16[512,1280]{1,0:T(8,128)(2,1)S(1)}, bf16[512,1280]{1,0:T(8,128)(2,1)S(1)}, u32[]{:S(2)}, u32[]{:S(2)}) collective-permute-start(bf16[512,1280]{1,0:T(8,128)(2,1)S(1)} %add_convert_fusion.1), channel_id=1, source_target_pairs={{8,4},{9,5},{10,6},{11,7},{12,8},{13,9},{14,10},{15,11},{24,20},{2... | collective-permute-start | bytes 3932168 | tf_op jit(solution)/shard_map/ppermute | solution.py:161
  219.8 54.7 %collective-permute-start.16 = (bf16[512,1280]{1,0:T(8,128)(2,1)S(1)}, bf16[512,1280]{1,0:T(8,128)(2,1)S(1)}, u32[]{:S(2)}, u32[]{:S(2)}) collective-permute-start(bf16[512,1280]{1,0:T(8,128)(2,1)S(1)} %add_convert_fusion.4), channel_id=1, source_target_pairs={{4,0},{5,1},{6,2},{7,3},{8,4},{9,5},{10,6},{11,7},{12,8},{13,9},{1... | collective-permute-start | bytes 3932168 | tf_op jit(solution)/shard_map/ppermute | solution.py:161
  222.5 56.4 %collective-permute-start.19 = (bf16[512,1280]{1,0:T(8,128)(2,1)S(1)}, bf16[512,1280]{1,0:T(8,128)(2,1)S(1)}, u32[]{:S(2)}, u32[]{:S(2)}) collective-permute-start(bf16[512,1280]{1,0:T(8,128)(2,1)S(1)} %get-tuple-element.17), channel_id=1, source_target_pairs={{0,4},{1,5},{2,6},{3,7},{4,8},{5,9},{6,10},{7,11},{8,12},{9,13},{1... | collective-permute-start | bytes 3932168 | tf_op jit(solution)/shard_map/ppermute | solution.py:161
  251.5 23.0 %copy-start.6 = (bf16[2048,1024]{1,0:T(8,128)(2,1)S(1)}, bf16[2048,1024]{1,0:T(8,128)(2,1)}, u32[]{:S(2)}) copy-start(bf16[2048,1024]{1,0:T(8,128)(2,1)} %get-tuple-element.8) | copy-start | bytes 12582916
  251.5 23.0 %copy-start.30 = (bf16[2048,128]{1,0:T(8,128)(2,1)S(1)}, bf16[2048,128]{1,0:T(8,128)(2,1)}, u32[]{:S(2)}) copy-start(bf16[2048,128]{1,0:T(8,128)(2,1)} %get-tuple-element.38) | copy-start | bytes 1572868
  251.5 23.0 %copy-start.32 = (bf16[2048,128]{1,0:T(8,128)(2,1)S(1)}, bf16[2048,128]{1,0:T(8,128)(2,1)}, u32[]{:S(2)}) copy-start(bf16[2048,128]{1,0:T(8,128)(2,1)} %get-tuple-element.76) | copy-start | bytes 1572868
  251.8 51.0 %collective-permute-start.22 = (bf16[512,1280]{1,0:T(8,128)(2,1)S(1)}, bf16[512,1280]{1,0:T(8,128)(2,1)S(1)}, u32[]{:S(2)}, u32[]{:S(2)}) collective-permute-start(bf16[512,1280]{1,0:T(8,128)(2,1)S(1)} %add_convert_fusion), channel_id=1, source_target_pairs={{4,0},{5,1},{6,2},{7,3},{8,4},{9,5},{10,6},{11,7},{12,8},{13,9},{1... | collective-permute-start | bytes 3932168 | tf_op jit(solution)/shard_map/ppermute | solution.py:161
  278.2 24.6 %copy-start.4 = (bf16[2048,1024]{1,0:T(8,128)(2,1)S(1)}, bf16[2048,1024]{1,0:T(8,128)(2,1)}, u32[]{:S(2)}) copy-start(bf16[2048,1024]{1,0:T(8,128)(2,1)} %get-tuple-element.7) | copy-start | bytes 12582916
  278.2 24.6 %copy-start.26 = (bf16[2048,128]{1,0:T(8,128)(2,1)S(1)}, bf16[2048,128]{1,0:T(8,128)(2,1)}, u32[]{:S(2)}) copy-start(bf16[2048,128]{1,0:T(8,128)(2,1)} %get-tuple-element.37) | copy-start | bytes 1572868
  278.2 24.6 %copy-start.28 = (bf16[2048,128]{1,0:T(8,128)(2,1)S(1)}, bf16[2048,128]{1,0:T(8,128)(2,1)}, u32[]{:S(2)}) copy-start(bf16[2048,128]{1,0:T(8,128)(2,1)} %get-tuple-element.77) | copy-start | bytes 1572868
  315.2 45.5 %slice-start = ((s8[8388608]{0:T(1024)(128)(4,1)}), s8[4194304]{0:T(1024)(128)(4,1)S(1)}, s32[]{:S(2)}) async-start(s8[8388608]{0:T(1024)(128)(4,1)} %bitcast.149), calls=%async_computation | async-start | bytes 8388608
  318.4 42.3 %slice-start.1 = ((s8[8388608]{0:T(1024)(128)(4,1)}), s8[4194304]{0:T(1024)(128)(4,1)S(1)}, s32[]{:S(2)}) async-start(s8[8388608]{0:T(1024)(128)(4,1)} %bitcast.149), calls=%async_computation.1 | async-start | bytes 8388608
  318.5 52.3 %collective-permute-start.31 = (bf16[512,1024]{0,1:T(8,128)(2,1)S(1)}, bf16[512,1024]{0,1:T(8,128)(2,1)}, u32[]{:S(2)}, u32[]{:S(2)}) collective-permute-start(bf16[512,1024]{0,1:T(8,128)(2,1)S(1)} %bitcast.177), channel_id=1, source_target_pairs={{4,0},{5,1},{6,2},{7,3},{8,4},{9,5},{10,6},{11,7},{12,8},{13,9},{1... | collective-permute-start | bytes 3145736 | tf_op jit(solution)/shard_map/ppermute | solution.py:161
  320.0 74.4 %collective-permute-start.29 = (bf16[512,1024]{0,1:T(8,128)(2,1)S(1)}, bf16[512,1024]{0,1:T(8,128)(2,1)}, u32[]{:S(2)}, u32[]{:S(2)}) collective-permute-start(bf16[512,1024]{0,1:T(8,128)(2,1)S(1)} %bitcast.178), channel_id=1, source_target_pairs={{0,4},{1,5},{2,6},{3,7},{4,8},{5,9},{6,10},{7,11},{8,12},{9,13},{1... | collective-permute-start | bytes 3145736 | tf_op jit(solution)/shard_map/ppermute | solution.py:161
  351.6 41.5 %collective-permute-start.27 = (bf16[512,1024]{0,1:T(8,128)(2,1)S(1)}, bf16[512,1024]{0,1:T(8,128)(2,1)S(1)}, u32[]{:S(2)}, u32[]{:S(2)}) collective-permute-start(bf16[512,1024]{0,1:T(8,128)(2,1)S(1)} %bitcast.180), channel_id=1, source_target_pairs={{4,0},{5,1},{6,2},{7,3},{8,4},{9,5},{10,6},{11,7},{12,8},{13,9},{1... | collective-permute-start | bytes 3145736 | tf_op jit(solution)/shard_map/ppermute | solution.py:161
  352.9 43.2 %collective-permute-start.25 = (bf16[512,1024]{0,1:T(8,128)(2,1)S(1)}, bf16[512,1024]{0,1:T(8,128)(2,1)S(1)}, u32[]{:S(2)}, u32[]{:S(2)}) collective-permute-start(bf16[512,1024]{0,1:T(8,128)(2,1)S(1)} %bitcast.181), channel_id=1, source_target_pairs={{0,4},{1,5},{2,6},{3,7},{4,8},{5,9},{6,10},{7,11},{8,12},{9,13},{1... | collective-permute-start | bytes 3145736 | tf_op jit(solution)/shard_map/ppermute | solution.py:161
  369.0 27.9 %collective-permute-start.23 = (bf16[2,128,2048]{2,1,0:T(8,128)(2,1)}, bf16[2,128,2048]{2,1,0:T(8,128)(2,1)}, u32[]{:S(2)}, u32[]{:S(2)}) collective-permute-start(bf16[2,128,2048]{2,1,0:T(8,128)(2,1)} %pad_maximum_fusion.10), channel_id=1, source_target_pairs={{0,1},{1,0},{2,3},{3,2},{4,5},{5,4},{6,7},{7,6},{8,9},{9,8},{10,11... | collective-permute-start | bytes 3145736 | tf_op jit(solution)/shard_map/ppermute | solution.py:14
  370.8 44.9 %collective-permute-start.32 = (bf16[512,1024]{0,1:T(8,128)(2,1)}, bf16[512,1024]{0,1:T(8,128)(2,1)}, u32[]{:S(2)}, u32[]{:S(2)}) collective-permute-start(bf16[512,1024]{0,1:T(8,128)(2,1)} %collective-permute-done.31), channel_id=1, source_target_pairs={{4,0},{5,1},{6,2},{7,3},{8,4},{9,5},{10,6},{11,7},{20,16},{21,17},... | collective-permute-start | bytes 3145736 | tf_op jit(solution)/shard_map/ppermute | solution.py:161
  393.1 45.0 %collective-permute-start.28 = (bf16[512,1024]{0,1:T(8,128)(2,1)S(1)}, bf16[512,1024]{0,1:T(8,128)(2,1)}, u32[]{:S(2)}, u32[]{:S(2)}) collective-permute-start(bf16[512,1024]{0,1:T(8,128)(2,1)S(1)} %collective-permute-done.27), channel_id=1, source_target_pairs={{4,0},{5,1},{6,2},{7,3},{8,4},{9,5},{10,6},{11,7},{20,16},{21,17},... | collective-permute-start | bytes 3145736 | tf_op jit(solution)/shard_map/ppermute | solution.py:161
  394.4 45.0 %collective-permute-start.30 = (bf16[512,1024]{0,1:T(8,128)(2,1)}, bf16[512,1024]{0,1:T(8,128)(2,1)}, u32[]{:S(2)}, u32[]{:S(2)}) collective-permute-start(bf16[512,1024]{0,1:T(8,128)(2,1)} %collective-permute-done.29), channel_id=1, source_target_pairs={{4,8},{5,9},{6,10},{7,11},{8,12},{9,13},{10,14},{11,15},{20,24},{2... | collective-permute-start | bytes 3145736 | tf_op jit(solution)/shard_map/ppermute | solution.py:161
  396.1 48.5 %collective-permute-start.26 = (bf16[512,1024]{0,1:T(8,128)(2,1)S(1)}, bf16[512,1024]{0,1:T(8,128)(2,1)S(1)}, u32[]{:S(2)}, u32[]{:S(2)}) collective-permute-start(bf16[512,1024]{0,1:T(8,128)(2,1)S(1)} %collective-permute-done.25), channel_id=1, source_target_pairs={{4,8},{5,9},{6,10},{7,11},{8,12},{9,13},{10,14},{11,15},{20,24},{2... | collective-permute-start | bytes 3145736 | tf_op jit(solution)/shard_map/ppermute | solution.py:161
  415.7 44.8 %collective-permute-start.42 = (bf16[512,1024]{0,1:T(8,128)(2,1)}, bf16[512,1024]{0,1:T(8,128)(2,1)S(1)}, u32[]{:S(2)}, u32[]{:S(2)}) collective-permute-start(bf16[512,1024]{0,1:T(8,128)(2,1)} %collective-permute-done.32), channel_id=1, source_target_pairs={{4,0},{5,1},{6,2},{7,3},{20,16},{21,17},{22,18},{23,19}} | collective-permute-start | bytes 3145736 | tf_op jit(solution)/shard_map/ppermute | solution.py:161
  438.2 42.9 %collective-permute-start.41 = (bf16[512,1024]{0,1:T(8,128)(2,1)}, bf16[512,1024]{0,1:T(8,128)(2,1)S(1)}, u32[]{:S(2)}, u32[]{:S(2)}) collective-permute-start(bf16[512,1024]{0,1:T(8,128)(2,1)} %collective-permute-done.28), channel_id=1, source_target_pairs={{4,0},{5,1},{6,2},{7,3},{20,16},{21,17},{22,18},{23,19}} | collective-permute-start | bytes 3145736 | tf_op jit(solution)/shard_map/ppermute | solution.py:161
  439.5 21.1 %slice-start.2 = ((s8[8388608]{0:T(1024)(128)(4,1)}), s8[4194304]{0:T(1024)(128)(4,1)S(1)}, s32[]{:S(2)}) async-start(s8[8388608]{0:T(1024)(128)(4,1)} %bitcast.151), calls=%async_computation.2 | async-start | bytes 8388608
  444.6 15.9 %slice-start.3 = ((s8[8388608]{0:T(1024)(128)(4,1)}), s8[4194304]{0:T(1024)(128)(4,1)S(1)}, s32[]{:S(2)}) async-start(s8[8388608]{0:T(1024)(128)(4,1)} %bitcast.151), calls=%async_computation.3 | async-start | bytes 8388608
  451.0 39.7 %collective-permute-start.33 = (bf16[2,128,2048]{2,1,0:T(8,128)(2,1)}, bf16[2,128,2048]{2,1,0:T(8,128)(2,1)S(1)}, u32[]{:S(2)}, u32[]{:S(2)}) collective-permute-start(bf16[2,128,2048]{2,1,0:T(8,128)(2,1)} %pad_maximum_fusion.11), channel_id=1, source_target_pairs={{0,1},{1,0},{2,3},{3,2},{4,5},{5,4},{6,7},{7,6},{8,9},{9,8},{10,11... | collective-permute-start | bytes 3145736 | tf_op jit(solution)/shard_map/ppermute | solution.py:14
  451.0 32.8 %collective-permute-start.37 = (bf16[512,1024]{0,1:T(8,128)(2,1)}, bf16[512,1024]{0,1:T(8,128)(2,1)S(1)}, u32[]{:S(2)}, u32[]{:S(2)}) collective-permute-start(bf16[512,1024]{0,1:T(8,128)(2,1)} %collective-permute-done.30), channel_id=1, source_target_pairs={{8,12},{9,13},{10,14},{11,15},{24,28},{25,29},{26,30},{27,31}} | collective-permute-start | bytes 3145736 | tf_op jit(solution)/shard_map/ppermute | solution.py:161
  451.8 35.7 %collective-permute-start.36 = (bf16[512,1024]{0,1:T(8,128)(2,1)S(1)}, bf16[512,1024]{0,1:T(8,128)(2,1)}, u32[]{:S(2)}, u32[]{:S(2)}) collective-permute-start(bf16[512,1024]{0,1:T(8,128)(2,1)S(1)} %collective-permute-done.26), channel_id=1, source_target_pairs={{8,12},{9,13},{10,14},{11,15},{24,28},{25,29},{26,30},{27,31}} | collective-permute-start | bytes 3145736 | tf_op jit(solution)/shard_map/ppermute | solution.py:161
  483.7 10.3 %collective-permute-start.43 = (bf16[2,128,2048]{2,1,0:T(8,128)(2,1)S(1)}, bf16[2,128,2048]{2,1,0:T(8,128)(2,1)S(1)}, u32[]{:S(2)}, u32[]{:S(2)}) collective-permute-start(bf16[2,128,2048]{2,1,0:T(8,128)(2,1)S(1)} %pad_maximum_fusion.13), channel_id=1, source_target_pairs={{0,1},{1,0},{2,3},{3,2},{4,5},{5,4},{6,7},{7,6},{8,9},{9,8},{10,11... | collective-permute-start | bytes 3145736 | tf_op jit(solution)/shard_map/ppermute | solution.py:14
  490.2 28.6 %collective-permute-start.38 = (bf16[2,128,2048]{2,1,0:T(8,128)(2,1)S(1)}, bf16[2,128,2048]{2,1,0:T(8,128)(2,1)S(1)}, u32[]{:S(2)}, u32[]{:S(2)}) collective-permute-start(bf16[2,128,2048]{2,1,0:T(8,128)(2,1)S(1)} %pad_maximum_fusion.12), channel_id=1, source_target_pairs={{0,1},{1,0},{2,3},{3,2},{4,5},{5,4},{6,7},{7,6},{8,9},{9,8},{10,11... | collective-permute-start | bytes 3145736 | tf_op jit(solution)/shard_map/ppermute | solution.py:14
  491.1 14.8 %collective-permute-start.34 = (bf16[128,2048]{1,0:T(8,128)(2,1)S(1)}, bf16[128,2048]{1,0:T(8,128)(2,1)S(1)}, u32[]{:S(2)}, u32[]{:S(2)}) collective-permute-start(bf16[128,2048]{1,0:T(8,128)(2,1)S(1)} %fusion.40), channel_id=1, source_target_pairs={{0,2},{1,3},{2,0},{3,1},{4,6},{5,7},{6,4},{7,5},{8,10},{9,11},{10,... | collective-permute-start | bytes 1572872 | tf_op jit(solution)/shard_map/ppermute | solution.py:14
  492.8 52.0 %collective-permute-start.24 = (bf16[128,2048]{1,0:T(8,128)(2,1)S(1)}, bf16[128,2048]{1,0:T(8,128)(2,1)S(1)}, u32[]{:S(2)}, u32[]{:S(2)}) collective-permute-start(bf16[128,2048]{1,0:T(8,128)(2,1)S(1)} %fusion.45), channel_id=1, source_target_pairs={{0,2},{1,3},{2,0},{3,1},{4,6},{5,7},{6,4},{7,5},{8,10},{9,11},{10,... | collective-permute-start | bytes 1572872 | tf_op jit(solution)/shard_map/ppermute | solution.py:14
  494.4 34.0 %collective-permute-start.44 = (bf16[128,2048]{1,0:T(8,128)(2,1)S(1)}, bf16[128,2048]{1,0:T(8,128)(2,1)S(1)}, u32[]{:S(2)}, u32[]{:S(2)}) collective-permute-start(bf16[128,2048]{1,0:T(8,128)(2,1)S(1)} %fusion.30), channel_id=1, source_target_pairs={{0,2},{1,3},{2,0},{3,1},{4,6},{5,7},{6,4},{7,5},{8,10},{9,11},{10,... | collective-permute-start | bytes 1572872 | tf_op jit(solution)/shard_map/ppermute | solution.py:14
  506.1 39.0 %collective-permute-start.35 = (bf16[128,2048]{1,0:T(8,128)(2,1)S(1)}, bf16[128,2048]{1,0:T(8,128)(2,1)S(1)}, u32[]{:S(2)}, u32[]{:S(2)}) collective-permute-start(bf16[128,2048]{1,0:T(8,128)(2,1)S(1)} %fusion.43), channel_id=1, source_target_pairs={{0,8},{1,9},{2,10},{3,11},{4,12},{5,13},{6,14},{7,15},{8,0},{9,1},... | collective-permute-start | bytes 1572872 | tf_op jit(solution)/shard_map/ppermute | solution.py:161
  519.2 25.3 %collective-permute-start.39 = (bf16[128,2048]{1,0:T(8,128)(2,1)S(1)}, bf16[128,2048]{1,0:T(8,128)(2,1)S(1)}, u32[]{:S(2)}, u32[]{:S(2)}) collective-permute-start(bf16[128,2048]{1,0:T(8,128)(2,1)S(1)} %fusion.35), channel_id=1, source_target_pairs={{0,2},{1,3},{2,0},{3,1},{4,6},{5,7},{6,4},{7,5},{8,10},{9,11},{10,... | collective-permute-start | bytes 1572872 | tf_op jit(solution)/shard_map/ppermute | solution.py:14
  528.6 38.6 %collective-permute-start.45 = (bf16[128,2048]{1,0:T(8,128)(2,1)S(1)}, bf16[128,2048]{1,0:T(8,128)(2,1)S(1)}, u32[]{:S(2)}, u32[]{:S(2)}) collective-permute-start(bf16[128,2048]{1,0:T(8,128)(2,1)S(1)} %fusion.33), channel_id=1, source_target_pairs={{0,12},{1,13},{2,14},{3,15},{4,0},{5,1},{6,2},{7,3},{8,4},{9,5},{1... | collective-permute-start | bytes 1572872 | tf_op jit(solution)/shard_map/ppermute | solution.py:161
  544.7 22.5 %collective-permute-start.40 = (bf16[128,2048]{1,0:T(8,128)(2,1)S(1)}, bf16[128,2048]{1,0:T(8,128)(2,1)S(1)}, u32[]{:S(2)}, u32[]{:S(2)}) collective-permute-start(bf16[128,2048]{1,0:T(8,128)(2,1)S(1)} %fusion.38), channel_id=1, source_target_pairs={{0,4},{1,5},{2,6},{3,7},{4,8},{5,9},{6,10},{7,11},{8,12},{9,13},{1... | collective-permute-start | bytes 1572872 | tf_op jit(solution)/shard_map/ppermute | solution.py:161
  (21 other events, 119.8 us)

commit v2 on v1

--- a/solution.py
+++ b/solution.py
@@ -233,45 +233,80 @@
     step = columns // PIECES
     right = [(z, z + 1) for z in range(ring - 1)]
     left = [(z + 1, z) for z in range(ring - 1)]
-    totals = [None] * ring
-    keys = values = None
+    kept = {}
+    weights = []
     for piece in range(PIECES):
-        has_kv = piece % repeats == 0
         weight = query_tiles[:, piece * step : (piece + 1) * step]
-        if has_kv:
+        if piece % repeats == 0:
             kv = piece // repeats
             span = slice(kv * HEAD_SIZE, (kv + 1) * HEAD_SIZE)
             weight = jnp.concatenate(
                 [weight, key_weight_tiles[:, span], value_weight_tiles[:, span]], axis=1
             )
-
-        def part(r):
-            return jnp.dot(slots[r], weight, preferred_element_type=jnp.float32)
-
-        going_right, going_left = part(1), part(3)
-        middle = None
-        for k in range(1, ring):
-            arrived_right = hop(going_right.astype(jnp.bfloat16), right[:k])
-            arrived_left = hop(going_left.astype(jnp.bfloat16), left[ring - 1 - k :])
-            if k < ring - 1:
-                going_right = part(k + 1) + arrived_right.astype(jnp.float32)
-                going_left = part(ring - 1 - k) + arrived_left.astype(jnp.float32)
-        summed = part(0) + arrived_right.astype(jnp.float32) + arrived_left.astype(jnp.float32)
-        if has_kv:
+        weights.append(weight)
+
+    def part(piece, r):
+        product = jnp.dot(slots[r], weights[piece], preferred_element_type=jnp.float32)
+        return lax.optimization_barrier(product)
+
+    def attend(piece, summed):
+        if piece % repeats == 0:
             keys = rotated(summed[:, step : step + HEAD_SIZE], cosine, sine).astype(jnp.bfloat16)
-            values = summed[:, step + HEAD_SIZE :].astype(jnp.bfloat16)
+            kept[piece // repeats] = keys, summed[:, step + HEAD_SIZE :].astype(jnp.bfloat16)
+        keys, values = kept[piece // repeats]
         queries = rotated(
             summed[:, :step].reshape(rows, -1, HEAD_SIZE), cosine[:, None], sine[:, None]
         )
         queries = (queries * HEAD_SIZE ** (-0.5)).astype(jnp.bfloat16)
-        own = attention(queries, keys, values, allowed)
-        from_left, from_right = [own], [own]
-        for k in range(1, ring):
-            from_left.append(hop(from_left[-1], right[k - 1 :]))
-            from_right.append(hop(from_right[-1], left[: ring - k]))
-        out_rows = output_tiles[piece * step : (piece + 1) * step]
-        for r in range(ring):
-            block = own if r == 0 else jnp.where(plane >= r, from_left[r], from_right[ring - r])
+        return attention(queries, keys, values, allowed)
+
+    totals = [None] * ring
+    arrived, summed = {}, {}
+    from_left = [[] for _ in range(PIECES)]
+    from_right = [[] for _ in range(PIECES)]
+    hops = ring - 1
+    for tick in range(1, hops * PIECES + 2 + hops):
+        payloads, receivers = [], []
+        attending = None
+        for piece in range(PIECES):
+            k = tick - hops * piece
+            if 1 <= k <= hops:
+                going_right, going_left = part(piece, k), part(piece, ring - k)
+                if k > 1:
+                    going_right += arrived[piece][0].astype(jnp.float32)
+                    going_left += arrived[piece][1].astype(jnp.float32)
+                payloads += [going_right.astype(jnp.bfloat16), going_left.astype(jnp.bfloat16)]
+                receivers.append(("sum", piece, k))
+            if k == ring:
+                own = part(piece, 0)
+                for value in arrived[piece]:
+                    own += value.astype(jnp.float32)
+                attending = piece
+                payloads.insert(0, own)
+            k = k - ring
+            if 1 <= k <= hops:
+                payloads += [from_left[piece][-1], from_right[piece][-1]]
+                receivers.append(("gather", piece, k))
+        payloads = list(lax.optimization_barrier(tuple(payloads)))
+        if attending is not None:
+            own = attend(attending, payloads.pop(0))
+            from_left[attending].append(own)
+            from_right[attending].append(own)
+        for kind, piece, k in receivers:
+            first, second = payloads.pop(0), payloads.pop(0)
+            if kind == "sum":
+                arrived[piece] = hop(first, right[:k]), hop(second, left[hops - k :])
+            else:
+                from_left[piece].append(hop(first, right[k - 1 :]))
+                from_right[piece].append(hop(second, left[: ring - k]))
+    for r in range(ring):
+        for piece in range(PIECES):
+            block = from_left[piece][0]
+            if r > 0:
+                block = jnp.where(
+                    plane >= r, from_left[piece][r], from_right[piece][ring - r]
+                )
+            out_rows = output_tiles[piece * step : (piece + 1) * step]
             product = jnp.dot(block, out_rows, preferred_element_type=jnp.float32)
             totals[r] = product if totals[r] is None else totals[r] + product
 

time: 579 us -> 520 us (0.90)
  starting transfers between devices: 161 us -> 75.7 us
  waiting for transfers between devices: 296 us -> 331 us
  matrix products: 72.8 us -> 62.6 us
    ppermute x30, starting transfers between devices: 150 us -> 66.8 us  [hop(): return lax.ppermute(value, 'mp', full)]
    ppermute x30, waiting for transfers between devices: 258 us -> 277 us  [hop(): return lax.ppermute(value, 'mp', full)]
    ppermute x16, waiting for transfers between devices: 37.7 us -> 54.8 us  [partner_2(): return lax.ppermute(value, axis, pairs)]
    dot_general x8, matrix products: 34 us -> 23.1 us  [part(): jnp.dot(slots[r], weights[piece], preferred_element_type=jnp.float32)]
  transfers between devices with their start and end apart: 46 -> 46, of which waited for: 19 -> 22; matrix products, arithmetic and copies ran while one was open for 15% -> 16% of each run, Pallas kernels for 0% -> 0%
where the time goes in v2:
time: 520 us; the launch traced here: 512 us
  waiting for transfers between devices  331 us (64%)
  starting transfers between devices  75.7 us (15%)
  matrix products  62.6 us (12%)
  local copies, waits for them, and re-layouts  20.3 us (4%)
  other arithmetic  20 us (4%)
    ppermute x30, waiting for transfers between devices, hop(): return lax.ppermute(value, 'mp', full)  277 us
    ppermute x30, starting transfers between devices, hop(): return lax.ppermute(value, 'mp', full)  66.8 us
    ppermute x16, waiting for transfers between devices, partner_2(): return lax.ppermute(value, axis, pairs)  54.8 us
    dot_general x8, matrix products, resident_weight_shards(): product = jnp.dot(block, out_rows, preferred_element_type=jnp.float32)  29.6 us
    dot_general x8, matrix products, part(): jnp.dot(slots[r], weights[piece], preferred_element_type=jnp.float32)  23.1 us
  transfers between devices with their start and end apart: 46, of which 22 were waited for; matrix products, arithmetic and copies ran while one was open for 16% of the time, Pallas kernels for 0%

profile of v2, /device:TPU:0, one launch (start us, length us, event | category | flops | bytes accessed | tf_op | source)
XLA Modules:
  0.0 511.6 jit_solution(10926998762786722742)
XLA Ops:
  0.0 2.2 fusion.2
  2.3 1.4 fusion.4
  4.9 3.0 collective-permute-start
  7.9 1.6 collective-permute-start.8
  9.4 2.2 collective-permute-start.2
  12.5 6.1 %fusion.103 = (bf16[2048,1024]{1,0:T(8,128)(2,1)}, bf16[2048,1024]{1,0:T(8,128)(2,1)}) fusion(bf16[2048,2048]{1,0:T(8,128)(2,1)} %param.10), kind=kLoop, calls=%fused_computation.184 | loop fusion | bytes 16777216 | tf_op jit(solution)/shard_map/slice | solution.py:239
  18.6 2.7 fusion.106
  23.4 1.4 collective-permute-done.8
  25.2 8.8 %collective-permute-done.2 = bf16[128,2048]{1,0:T(8,128)(2,1)S(1)} collective-permute-done((bf16[128,2048]{1,0:T(8,128)(2,1)}, bf16[128,2048]{1,0:T(8,128)(2,1)S(1)}, u32[]{:S(2)}, u32[]{:S(2)}) %collective-permute-start.2) | collective-permute-done | bytes 524320 | tf_op jit(solution)/shard_map/ppermute | solution.py:161
  34.8 22.3 %collective-permute-done.5 = bf16[128,2048]{1,0:T(8,128)(2,1)S(1)} collective-permute-done((bf16[128,2048]{1,0:T(8,128)(2,1)}, bf16[128,2048]{1,0:T(8,128)(2,1)S(1)}, u32[]{:S(2)}, u32[]{:S(2)}) %collective-permute-start.5) | collective-permute-done | bytes 524320 | tf_op jit(solution)/shard_map/ppermute | solution.py:161
  58.4 12.5 %collective-permute-done.6 = bf16[128,2048]{1,0:T(8,128)(2,1)S(1)} collective-permute-done((bf16[128,2048]{1,0:T(8,128)(2,1)S(1)}, bf16[128,2048]{1,0:T(8,128)(2,1)S(1)}, u32[]{:S(2)}, u32[]{:S(2)}) %collective-permute-start.6) | collective-permute-done | bytes 524320 | tf_op jit(solution)/shard_map/ppermute | solution.py:14
  72.7 1.3 copy-done.3
  74.0 2.9 fusion.99
  77.4 2.9 fusion.101
  80.4 8.9 %collective-permute-start.11 = (bf16[512,1280]{1,0:T(8,128)(2,1)S(1)}, bf16[512,1280]{1,0:T(8,128)(2,1)S(1)}, u32[]{:S(2)}, u32[]{:S(2)}) collective-permute-start(bf16[512,1280]{1,0:T(8,128)(2,1)S(1)} %convert_element_type.167), channel_id=1, source_target_pairs={{0,4},{1,5},{2,6},{3,7},{16,20},{17,21},{18,22},{19,23}} | collective-permute-start | bytes 3932168 | tf_op jit(solution)/shard_map/ppermute | solution.py:161
  90.7 2.9 fusion.100
  93.6 24.4 %collective-permute-done.11 = bf16[512,1280]{1,0:T(8,128)(2,1)S(1)} collective-permute-done((bf16[512,1280]{1,0:T(8,128)(2,1)S(1)}, bf16[512,1280]{1,0:T(8,128)(2,1)S(1)}, u32[]{:S(2)}, u32[]{:S(2)}) %collective-permute-start.11) | collective-permute-done | bytes 1310752 | tf_op jit(solution)/shard_map/ppermute | solution.py:161
  119.3 2.9 fusion.102
  122.2 5.0 collective-permute-start.13
  127.2 2.9 fusion.98
  130.5 24.5 %collective-permute-done.13 = bf16[512,1280]{1,0:T(8,128)(2,1)S(1)} collective-permute-done((bf16[512,1280]{1,0:T(8,128)(2,1)S(1)}, bf16[512,1280]{1,0:T(8,128)(2,1)S(1)}, u32[]{:S(2)}, u32[]{:S(2)}) %collective-permute-start.13) | collective-permute-done | bytes 1310752 | tf_op jit(solution)/shard_map/ppermute | solution.py:161
  155.3 5.7 %collective-permute-start.15 = (bf16[512,1280]{1,0:T(8,128)(2,1)S(1)}, bf16[512,1280]{1,0:T(8,128)(2,1)S(1)}, u32[]{:S(2)}, u32[]{:S(2)}) collective-permute-start(bf16[512,1280]{1,0:T(8,128)(2,1)S(1)} %add_convert_fusion.5), channel_id=1, source_target_pairs={{0,4},{1,5},{2,6},{3,7},{4,8},{5,9},{6,10},{7,11},{8,12},{9,13},{1... | collective-permute-start | bytes 3932168 | tf_op jit(solution)/shard_map/ppermute | solution.py:161
  162.3 2.9 fusion.97
  165.4 2.9 fusion.95
  168.2 19.7 %collective-permute-done.15 = bf16[512,1280]{1,0:T(8,128)(2,1)S(1)} collective-permute-done((bf16[512,1280]{1,0:T(8,128)(2,1)S(1)}, bf16[512,1280]{1,0:T(8,128)(2,1)S(1)}, u32[]{:S(2)}, u32[]{:S(2)}) %collective-permute-start.15) | collective-permute-done | bytes 1310752 | tf_op jit(solution)/shard_map/ppermute | solution.py:161
  187.9 4.9 collective-permute-done.16
  193.2 3.7 collective-permute-start.17
  201.5 2.3 fusion
  203.9 3.0 fusion.22
  206.9 15.7 %collective-permute-done.17 = bf16[512,1280]{1,0:T(8,128)(2,1)S(1)} collective-permute-done((bf16[512,1280]{1,0:T(8,128)(2,1)S(1)}, bf16[512,1280]{1,0:T(8,128)(2,1)S(1)}, u32[]{:S(2)}, u32[]{:S(2)}) %collective-permute-start.17) | collective-permute-done | bytes 1310752 | tf_op jit(solution)/shard_map/ppermute | solution.py:161
  223.9 5.0 collective-permute-start.21
  229.0 4.5 collective-permute-start.19
  235.1 23.0 %collective-permute-done.21 = bf16[512,1280]{1,0:T(8,128)(2,1)S(1)} collective-permute-done((bf16[512,1280]{1,0:T(8,128)(2,1)S(1)}, bf16[512,1280]{1,0:T(8,128)(2,1)S(1)}, u32[]{:S(2)}, u32[]{:S(2)}) %collective-permute-start.21) | collective-permute-done | bytes 1310752 | tf_op jit(solution)/shard_map/ppermute | solution.py:161
  258.4 18.0 %collective-permute-done.19 = bf16[512,1024]{0,1:T(8,128)(2,1)S(1)} collective-permute-done((bf16[512,1024]{0,1:T(8,128)(2,1)}, bf16[512,1024]{0,1:T(8,128)(2,1)S(1)}, u32[]{:S(2)}, u32[]{:S(2)}) %collective-permute-start.19) | collective-permute-done | bytes 1048608 | tf_op jit(solution)/shard_map/ppermute | solution.py:161
  276.3 4.4 collective-permute-start.23
  280.7 1.3 collective-permute-start.24
  282.0 2.9 fusion.96
  285.6 1.5 collective-permute-start.26
  287.1 3.6 fusion.17
  290.8 13.8 %collective-permute-done.23 = bf16[512,1280]{1,0:T(8,128)(2,1)S(1)} collective-permute-done((bf16[512,1280]{1,0:T(8,128)(2,1)S(1)}, bf16[512,1280]{1,0:T(8,128)(2,1)S(1)}, u32[]{:S(2)}, u32[]{:S(2)}) %collective-permute-start.23) | collective-permute-done | bytes 1310752 | tf_op jit(solution)/shard_map/ppermute | solution.py:161
  304.6 10.0 %collective-permute-done.24 = bf16[512,1280]{1,0:T(8,128)(2,1)S(1)} collective-permute-done((bf16[512,1280]{1,0:T(8,128)(2,1)S(1)}, bf16[512,1280]{1,0:T(8,128)(2,1)S(1)}, u32[]{:S(2)}, u32[]{:S(2)}) %collective-permute-start.24) | collective-permute-done | bytes 1310752 | tf_op jit(solution)/shard_map/ppermute | solution.py:161
  315.1 16.4 %collective-permute-done.26 = bf16[512,1024]{0,1:T(8,128)(2,1)S(1)} collective-permute-done((bf16[512,1024]{0,1:T(8,128)(2,1)S(1)}, bf16[512,1024]{0,1:T(8,128)(2,1)S(1)}, u32[]{:S(2)}, u32[]{:S(2)}) %collective-permute-start.26) | collective-permute-done | bytes 1048608 | tf_op jit(solution)/shard_map/ppermute | solution.py:161
  334.9 2.4 fusion.1
  337.4 2.1 fusion.21
  339.5 4.7 collective-permute-start.29
  345.5 4.6 fusion.112
  351.3 8.7 %collective-permute-done.29 = bf16[512,1024]{0,1:T(8,128)(2,1)} collective-permute-done((bf16[512,1024]{0,1:T(8,128)(2,1)S(1)}, bf16[512,1024]{0,1:T(8,128)(2,1)}, u32[]{:S(2)}, u32[]{:S(2)}) %collective-permute-start.29) | collective-permute-done | bytes 1048608 | tf_op jit(solution)/shard_map/ppermute | solution.py:161
  360.0 5.6 %collective-permute-done.30 = bf16[512,1024]{0,1:T(8,128)(2,1)} collective-permute-done((bf16[512,1024]{0,1:T(8,128)(2,1)S(1)}, bf16[512,1024]{0,1:T(8,128)(2,1)}, u32[]{:S(2)}, u32[]{:S(2)}) %collective-permute-start.30) | collective-permute-done | bytes 1048608 | tf_op jit(solution)/shard_map/ppermute | solution.py:161
  365.6 1.7 collective-permute-start.31
  370.7 1.5 convert_element_type.200
  372.2 23.5 %collective-permute-done.32 = bf16[512,1024]{0,1:T(8,128)(2,1)} collective-permute-done((bf16[512,1024]{0,1:T(8,128)(2,1)}, bf16[512,1024]{0,1:T(8,128)(2,1)}, u32[]{:S(2)}, u32[]{:S(2)}) %collective-permute-start.32) | collective-permute-done | bytes 1048608 | tf_op jit(solution)/shard_map/ppermute | solution.py:161
  396.9 1.9 collective-permute-start.37
  398.8 5.2 %fusion.11 = f32[512,2048]{1,0:T(8,128)S(1)} fusion(bf16[2048,2048]{1,0:T(8,128)(2,1)} %param.13, bf16[512,1024]{0,1:T(8,128)(2,1)} %collective-permute-done.31, bf16[512,1024]{0,1:T(8,128)(2,1)} %collective-permute-done.32, pred[]{:T(512)S(6)} %ge.12), kind=kOutput, calls=%fused_computation.23 | convolution fusion | flops 2148007936 | bytes 10485761 | tf_op jit(solution)/shard_map/dot_general | solution.py:310
  404.0 4.9 fusion.113
  410.0 22.6 %collective-permute-done.42 = bf16[512,1024]{0,1:T(8,128)(2,1)S(1)} collective-permute-done((bf16[512,1024]{0,1:T(8,128)(2,1)}, bf16[512,1024]{0,1:T(8,128)(2,1)S(1)}, u32[]{:S(2)}, u32[]{:S(2)}) %collective-permute-start.42) | collective-permute-done | bytes 1048608 | tf_op jit(solution)/shard_map/ppermute | solution.py:161
  432.6 2.4 fusion.7
  435.1 2.5 fusion.115
  438.7 3.7 fusion.9
  442.4 2.7 fusion.114
  450.2 11.0 %collective-permute-done.34 = bf16[128,2048]{1,0:T(8,128)(2,1)S(1)} collective-permute-done((bf16[128,2048]{1,0:T(8,128)(2,1)S(1)}, bf16[128,2048]{1,0:T(8,128)(2,1)S(1)}, u32[]{:S(2)}, u32[]{:S(2)}) %collective-permute-start.34) | collective-permute-done | bytes 524320 | tf_op jit(solution)/shard_map/ppermute | solution.py:14
  462.3 21.3 %collective-permute-done.44 = bf16[128,2048]{1,0:T(8,128)(2,1)S(1)} collective-permute-done((bf16[128,2048]{1,0:T(8,128)(2,1)S(1)}, bf16[128,2048]{1,0:T(8,128)(2,1)S(1)}, u32[]{:S(2)}, u32[]{:S(2)}) %collective-permute-start.44) | collective-permute-done | bytes 524320 | tf_op jit(solution)/shard_map/ppermute | solution.py:14
  483.8 10.1 %collective-permute-done.39 = bf16[128,2048]{1,0:T(8,128)(2,1)S(1)} collective-permute-done((bf16[128,2048]{1,0:T(8,128)(2,1)S(1)}, bf16[128,2048]{1,0:T(8,128)(2,1)S(1)}, u32[]{:S(2)}, u32[]{:S(2)}) %collective-permute-start.39) | collective-permute-done | bytes 524320 | tf_op jit(solution)/shard_map/ppermute | solution.py:14
  495.5 13.4 %collective-permute-done.40 = bf16[128,2048]{1,0:T(8,128)(2,1)S(1)} collective-permute-done((bf16[128,2048]{1,0:T(8,128)(2,1)S(1)}, bf16[128,2048]{1,0:T(8,128)(2,1)S(1)}, u32[]{:S(2)}, u32[]{:S(2)}) %collective-permute-start.40) | collective-permute-done | bytes 524320 | tf_op jit(solution)/shard_map/ppermute | solution.py:161
  509.0 1.3 copy-done.4
  (153 shorter events, 44.5 us)
Async XLA Ops:
  0.0 2.3 copy-start.1
  4.9 20.1 %collective-permute-start = (bf16[128,2048]{1,0:T(8,128)(2,1)S(1)}, bf16[128,2048]{1,0:T(8,128)(2,1)S(1)}, u32[]{:S(2)}, u32[]{:S(2)}) collective-permute-start(bf16[128,2048]{1,0:T(8,128)(2,1)S(1)} %get-tuple-element.83), channel_id=1, source_target_pairs={{0,2},{1,3},{2,0},{3,1},{4,6},{5,7},{6,4},{7,5},{8,10},{9,11},{10,... | collective-permute-start | bytes 1572872 | tf_op jit(solution)/shard_map/ppermute | solution.py:14
  7.9 16.9 %collective-permute-start.8 = (bf16[128,2048]{1,0:T(8,128)(2,1)}, bf16[128,2048]{1,0:T(8,128)(2,1)S(1)}, u32[]{:S(2)}, u32[]{:S(2)}) collective-permute-start(bf16[128,2048]{1,0:T(8,128)(2,1)} %get-tuple-element.84), channel_id=1, source_target_pairs={{0,4},{1,5},{2,6},{3,7},{4,8},{5,9},{6,10},{7,11},{8,12},{9,13},{1... | collective-permute-start | bytes 1572872 | tf_op jit(solution)/shard_map/ppermute | solution.py:161
  9.4 24.5 %collective-permute-start.2 = (bf16[128,2048]{1,0:T(8,128)(2,1)}, bf16[128,2048]{1,0:T(8,128)(2,1)S(1)}, u32[]{:S(2)}, u32[]{:S(2)}) collective-permute-start(bf16[128,2048]{1,0:T(8,128)(2,1)} %get-tuple-element.86), channel_id=1, source_target_pairs={{0,12},{1,13},{2,14},{3,15},{4,0},{5,1},{6,2},{7,3},{8,4},{9,5},{1... | collective-permute-start | bytes 1572872 | tf_op jit(solution)/shard_map/ppermute | solution.py:161
  11.7 45.3 %collective-permute-start.5 = (bf16[128,2048]{1,0:T(8,128)(2,1)}, bf16[128,2048]{1,0:T(8,128)(2,1)S(1)}, u32[]{:S(2)}, u32[]{:S(2)}) collective-permute-start(bf16[128,2048]{1,0:T(8,128)(2,1)} %get-tuple-element.85), channel_id=1, source_target_pairs={{0,8},{1,9},{2,10},{3,11},{4,12},{5,13},{6,14},{7,15},{8,0},{9,1},... | collective-permute-start | bytes 1572872 | tf_op jit(solution)/shard_map/ppermute | solution.py:161
  18.6 2.7 copy-start.10
  24.8 32.8 %collective-permute-start.9 = (bf16[128,2048]{1,0:T(8,128)(2,1)S(1)}, bf16[128,2048]{1,0:T(8,128)(2,1)S(1)}, u32[]{:S(2)}, u32[]{:S(2)}) collective-permute-start(bf16[128,2048]{1,0:T(8,128)(2,1)S(1)} %collective-permute-done.8), channel_id=1, source_target_pairs={{0,2},{1,3},{2,0},{3,1},{4,6},{5,7},{6,4},{7,5},{8,10},{9,11},{10,... | collective-permute-start | bytes 1572872 | tf_op jit(solution)/shard_map/ppermute | solution.py:14
  25.1 45.9 %collective-permute-start.1 = (bf16[2,128,2048]{2,1,0:T(8,128)(2,1)S(1)}, bf16[2,128,2048]{2,1,0:T(8,128)(2,1)S(1)}, u32[]{:S(2)}, u32[]{:S(2)}) collective-permute-start(bf16[2,128,2048]{2,1,0:T(8,128)(2,1)S(1)} %pad_maximum_fusion.6), channel_id=1, source_target_pairs={{0,1},{1,0},{2,3},{3,2},{4,5},{5,4},{6,7},{7,6},{8,9},{9,8},{10,11... | collective-permute-start | bytes 3145736 | tf_op jit(solution)/shard_map/ppermute | solution.py:14
  34.0 23.7 %collective-permute-start.3 = (bf16[128,2048]{1,0:T(8,128)(2,1)S(1)}, bf16[128,2048]{1,0:T(8,128)(2,1)S(1)}, u32[]{:S(2)}, u32[]{:S(2)}) collective-permute-start(bf16[128,2048]{1,0:T(8,128)(2,1)S(1)} %collective-permute-done.2), channel_id=1, source_target_pairs={{0,2},{1,3},{2,0},{3,1},{4,6},{5,7},{6,4},{7,5},{8,10},{9,11},{10,... | collective-permute-start | bytes 1572872 | tf_op jit(solution)/shard_map/ppermute | solution.py:14
  57.0 13.8 %collective-permute-start.6 = (bf16[128,2048]{1,0:T(8,128)(2,1)S(1)}, bf16[128,2048]{1,0:T(8,128)(2,1)S(1)}, u32[]{:S(2)}, u32[]{:S(2)}) collective-permute-start(bf16[128,2048]{1,0:T(8,128)(2,1)S(1)} %collective-permute-done.5), channel_id=1, source_target_pairs={{0,2},{1,3},{2,0},{3,1},{4,6},{5,7},{6,4},{7,5},{8,10},{9,11},{10,... | collective-permute-start | bytes 1572872 | tf_op jit(solution)/shard_map/ppermute | solution.py:14
  57.6 13.8 %collective-permute-start.10 = (bf16[2,128,2048]{2,1,0:T(8,128)(2,1)S(1)}, bf16[2,128,2048]{2,1,0:T(8,128)(2,1)S(1)}, u32[]{:S(2)}, u32[]{:S(2)}) collective-permute-start(bf16[2,128,2048]{2,1,0:T(8,128)(2,1)S(1)} %pad_maximum_fusion.9), channel_id=1, source_target_pairs={{0,1},{1,0},{2,3},{3,2},{4,5},{5,4},{6,7},{7,6},{8,9},{9,8},{10,11... | collective-permute-start | bytes 3145736 | tf_op jit(solution)/shard_map/ppermute | solution.py:14
  57.8 19.2 %collective-permute-start.4 = (bf16[2,128,2048]{2,1,0:T(8,128)(2,1)S(1)}, bf16[2,128,2048]{2,1,0:T(8,128)(2,1)S(1)}, u32[]{:S(2)}, u32[]{:S(2)}) collective-permute-start(bf16[2,128,2048]{2,1,0:T(8,128)(2,1)S(1)} %pad_maximum_fusion.7), channel_id=1, source_target_pairs={{0,1},{1,0},{2,3},{3,2},{4,5},{5,4},{6,7},{7,6},{8,9},{9,8},{10,11... | collective-permute-start | bytes 3145736 | tf_op jit(solution)/shard_map/ppermute | solution.py:14
  71.0 19.4 %collective-permute-start.7 = (bf16[2,128,2048]{2,1,0:T(8,128)(2,1)S(1)}, bf16[2,128,2048]{2,1,0:T(8,128)(2,1)S(1)}, u32[]{:S(2)}, u32[]{:S(2)}) collective-permute-start(bf16[2,128,2048]{2,1,0:T(8,128)(2,1)S(1)} %pad_maximum_fusion.8), channel_id=1, source_target_pairs={{0,1},{1,0},{2,3},{3,2},{4,5},{5,4},{6,7},{7,6},{8,9},{9,8},{10,11... | collective-permute-start | bytes 3145736 | tf_op jit(solution)/shard_map/ppermute | solution.py:14
  71.5 1.0 copy-start.8
  71.5 1.2 copy-start.9
  71.5 2.4 copy-start.3
  80.4 37.5 %collective-permute-start.11 = (bf16[512,1280]{1,0:T(8,128)(2,1)S(1)}, bf16[512,1280]{1,0:T(8,128)(2,1)S(1)}, u32[]{:S(2)}, u32[]{:S(2)}) collective-permute-start(bf16[512,1280]{1,0:T(8,128)(2,1)S(1)} %convert_element_type.167), channel_id=1, source_target_pairs={{0,4},{1,5},{2,6},{3,7},{16,20},{17,21},{18,22},{19,23}} | collective-permute-start | bytes 3932168 | tf_op jit(solution)/shard_map/ppermute | solution.py:161
  89.4 28.6 %collective-permute-start.12 = (bf16[512,1280]{1,0:T(8,128)(2,1)S(1)}, bf16[512,1280]{1,0:T(8,128)(2,1)S(1)}, u32[]{:S(2)}, u32[]{:S(2)}) collective-permute-start(bf16[512,1280]{1,0:T(8,128)(2,1)S(1)} %convert_element_type.168), channel_id=1, source_target_pairs={{12,8},{13,9},{14,10},{15,11},{28,24},{29,25},{30,26},{31,27}} | collective-permute-start | bytes 3932168 | tf_op jit(solution)/shard_map/ppermute | solution.py:161
  118.5 11.7 %collective-permute-start.14 = (bf16[512,1280]{1,0:T(8,128)(2,1)S(1)}, bf16[512,1280]{1,0:T(8,128)(2,1)S(1)}, u32[]{:S(2)}, u32[]{:S(2)}) collective-permute-start(bf16[512,1280]{1,0:T(8,128)(2,1)S(1)} %get-tuple-element.34), channel_id=1, source_target_pairs={{8,4},{9,5},{10,6},{11,7},{12,8},{13,9},{14,10},{15,11},{24,20},{2... | collective-permute-start | bytes 3932168 | tf_op jit(solution)/shard_map/ppermute | solution.py:161
  119.3 7.9 %copy-start.2 = (bf16[2048,1024]{1,0:T(8,128)(2,1)S(1)}, bf16[2048,1024]{1,0:T(8,128)(2,1)}, u32[]{:S(2)}) copy-start(bf16[2048,1024]{1,0:T(8,128)(2,1)} %get-tuple-element.57) | copy-start | bytes 12582916
  119.3 7.9 %copy-start.7 = (bf16[2048,128]{1,0:T(8,128)(2,1)S(1)}, bf16[2048,128]{1,0:T(8,128)(2,1)}, u32[]{:S(2)}) copy-start(bf16[2048,128]{1,0:T(8,128)(2,1)} %get-tuple-element.118) | copy-start | bytes 1572868
  122.2 32.8 %collective-permute-start.13 = (bf16[512,1280]{1,0:T(8,128)(2,1)S(1)}, bf16[512,1280]{1,0:T(8,128)(2,1)S(1)}, u32[]{:S(2)}, u32[]{:S(2)}) collective-permute-start(bf16[512,1280]{1,0:T(8,128)(2,1)S(1)} %get-tuple-element.33), channel_id=1, source_target_pairs={{0,4},{1,5},{2,6},{3,7},{4,8},{5,9},{6,10},{7,11},{16,20},{17,21},... | collective-permute-start | bytes 3932168 | tf_op jit(solution)/shard_map/ppermute | solution.py:161
  155.3 32.6 %collective-permute-start.15 = (bf16[512,1280]{1,0:T(8,128)(2,1)S(1)}, bf16[512,1280]{1,0:T(8,128)(2,1)S(1)}, u32[]{:S(2)}, u32[]{:S(2)}) collective-permute-start(bf16[512,1280]{1,0:T(8,128)(2,1)S(1)} %add_convert_fusion.5), channel_id=1, source_target_pairs={{0,4},{1,5},{2,6},{3,7},{4,8},{5,9},{6,10},{7,11},{8,12},{9,13},{1... | collective-permute-start | bytes 3932168 | tf_op jit(solution)/shard_map/ppermute | solution.py:161
  161.0 31.8 %collective-permute-start.16 = (bf16[512,1280]{1,0:T(8,128)(2,1)S(1)}, bf16[512,1280]{1,0:T(8,128)(2,1)S(1)}, u32[]{:S(2)}, u32[]{:S(2)}) collective-permute-start(bf16[512,1280]{1,0:T(8,128)(2,1)S(1)} %add_convert_fusion.4), channel_id=1, source_target_pairs={{4,0},{5,1},{6,2},{7,3},{8,4},{9,5},{10,6},{11,7},{12,8},{13,9},{1... | collective-permute-start | bytes 3932168 | tf_op jit(solution)/shard_map/ppermute | solution.py:161
  193.2 29.4 %collective-permute-start.17 = (bf16[512,1280]{1,0:T(8,128)(2,1)S(1)}, bf16[512,1280]{1,0:T(8,128)(2,1)S(1)}, u32[]{:S(2)}, u32[]{:S(2)}) collective-permute-start(bf16[512,1280]{1,0:T(8,128)(2,1)S(1)} %convert_element_type.179), channel_id=1, source_target_pairs={{0,4},{1,5},{2,6},{3,7},{16,20},{17,21},{18,22},{19,23}} | collective-permute-start | bytes 3932168 | tf_op jit(solution)/shard_map/ppermute | solution.py:161
  196.9 25.7 %collective-permute-start.18 = (bf16[512,1280]{1,0:T(8,128)(2,1)S(1)}, bf16[512,1280]{1,0:T(8,128)(2,1)S(1)}, u32[]{:S(2)}, u32[]{:S(2)}) collective-permute-start(bf16[512,1280]{1,0:T(8,128)(2,1)S(1)} %convert_element_type.180), channel_id=1, source_target_pairs={{12,8},{13,9},{14,10},{15,11},{28,24},{29,25},{30,26},{31,27}} | collective-permute-start | bytes 3932168 | tf_op jit(solution)/shard_map/ppermute | solution.py:161
  223.2 11.6 %collective-permute-start.22 = (bf16[512,1280]{1,0:T(8,128)(2,1)S(1)}, bf16[512,1280]{1,0:T(8,128)(2,1)S(1)}, u32[]{:S(2)}, u32[]{:S(2)}) collective-permute-start(bf16[512,1280]{1,0:T(8,128)(2,1)S(1)} %get-tuple-element.43), channel_id=1, source_target_pairs={{8,4},{9,5},{10,6},{11,7},{12,8},{13,9},{14,10},{15,11},{24,20},{2... | collective-permute-start | bytes 3932168 | tf_op jit(solution)/shard_map/ppermute | solution.py:161
  223.9 34.2 %collective-permute-start.21 = (bf16[512,1280]{1,0:T(8,128)(2,1)S(1)}, bf16[512,1280]{1,0:T(8,128)(2,1)S(1)}, u32[]{:S(2)}, u32[]{:S(2)}) collective-permute-start(bf16[512,1280]{1,0:T(8,128)(2,1)S(1)} %get-tuple-element.42), channel_id=1, source_target_pairs={{0,4},{1,5},{2,6},{3,7},{4,8},{5,9},{6,10},{7,11},{16,20},{17,21},... | collective-permute-start | bytes 3932168 | tf_op jit(solution)/shard_map/ppermute | solution.py:161
  229.0 47.4 %collective-permute-start.19 = (bf16[512,1024]{0,1:T(8,128)(2,1)}, bf16[512,1024]{0,1:T(8,128)(2,1)S(1)}, u32[]{:S(2)}, u32[]{:S(2)}) collective-permute-start(bf16[512,1024]{0,1:T(8,128)(2,1)} %bitcast.21), channel_id=1, source_target_pairs={{0,4},{1,5},{2,6},{3,7},{4,8},{5,9},{6,10},{7,11},{8,12},{9,13},{1... | collective-permute-start | bytes 3145736 | tf_op jit(solution)/shard_map/ppermute | solution.py:161
  233.5 42.8 %collective-permute-start.20 = (bf16[512,1024]{0,1:T(8,128)(2,1)}, bf16[512,1024]{0,1:T(8,128)(2,1)S(1)}, u32[]{:S(2)}, u32[]{:S(2)}) collective-permute-start(bf16[512,1024]{0,1:T(8,128)(2,1)} %bitcast.21), channel_id=1, source_target_pairs={{4,0},{5,1},{6,2},{7,3},{8,4},{9,5},{10,6},{11,7},{12,8},{13,9},{1... | collective-permute-start | bytes 3145736 | tf_op jit(solution)/shard_map/ppermute | solution.py:161
  258.1 29.0 %slice-start = ((s8[8388608]{0:T(1024)(128)(4,1)}), s8[4194304]{0:T(1024)(128)(4,1)S(1)}, s32[]{:S(2)}) async-start(s8[8388608]{0:T(1024)(128)(4,1)} %bitcast.151), calls=%async_computation | async-start | bytes 8388608
  258.4 28.7 %slice-start.1 = ((s8[8388608]{0:T(1024)(128)(4,1)}), s8[4194304]{0:T(1024)(128)(4,1)S(1)}, s32[]{:S(2)}) async-start(s8[8388608]{0:T(1024)(128)(4,1)} %bitcast.151), calls=%async_computation.1 | async-start | bytes 8388608
  276.3 28.2 %collective-permute-start.23 = (bf16[512,1280]{1,0:T(8,128)(2,1)S(1)}, bf16[512,1280]{1,0:T(8,128)(2,1)S(1)}, u32[]{:S(2)}, u32[]{:S(2)}) collective-permute-start(bf16[512,1280]{1,0:T(8,128)(2,1)S(1)} %add_convert_fusion.1), channel_id=1, source_target_pairs={{0,4},{1,5},{2,6},{3,7},{4,8},{5,9},{6,10},{7,11},{8,12},{9,13},{1... | collective-permute-start | bytes 3932168 | tf_op jit(solution)/shard_map/ppermute | solution.py:161
  280.7 33.9 %collective-permute-start.24 = (bf16[512,1280]{1,0:T(8,128)(2,1)S(1)}, bf16[512,1280]{1,0:T(8,128)(2,1)S(1)}, u32[]{:S(2)}, u32[]{:S(2)}) collective-permute-start(bf16[512,1280]{1,0:T(8,128)(2,1)S(1)} %add_convert_fusion), channel_id=1, source_target_pairs={{4,0},{5,1},{6,2},{7,3},{8,4},{9,5},{10,6},{11,7},{12,8},{13,9},{1... | collective-permute-start | bytes 3932168 | tf_op jit(solution)/shard_map/ppermute | solution.py:161
  284.9 30.2 %collective-permute-start.25 = (bf16[512,1024]{0,1:T(8,128)(2,1)S(1)}, bf16[512,1024]{0,1:T(8,128)(2,1)S(1)}, u32[]{:S(2)}, u32[]{:S(2)}) collective-permute-start(bf16[512,1024]{0,1:T(8,128)(2,1)S(1)} %collective-permute-done.19), channel_id=1, source_target_pairs={{4,8},{5,9},{6,10},{7,11},{8,12},{9,13},{10,14},{11,15},{20,24},{2... | collective-permute-start | bytes 3145736 | tf_op jit(solution)/shard_map/ppermute | solution.py:161
  285.6 45.9 %collective-permute-start.26 = (bf16[512,1024]{0,1:T(8,128)(2,1)S(1)}, bf16[512,1024]{0,1:T(8,128)(2,1)S(1)}, u32[]{:S(2)}, u32[]{:S(2)}) collective-permute-start(bf16[512,1024]{0,1:T(8,128)(2,1)S(1)} %collective-permute-done.20), channel_id=1, source_target_pairs={{4,0},{5,1},{6,2},{7,3},{8,4},{9,5},{10,6},{11,7},{20,16},{21,17},... | collective-permute-start | bytes 3145736 | tf_op jit(solution)/shard_map/ppermute | solution.py:161
  331.5 2.7 copy-start.5
  339.5 20.5 %collective-permute-start.29 = (bf16[512,1024]{0,1:T(8,128)(2,1)S(1)}, bf16[512,1024]{0,1:T(8,128)(2,1)}, u32[]{:S(2)}, u32[]{:S(2)}) collective-permute-start(bf16[512,1024]{0,1:T(8,128)(2,1)S(1)} %bitcast.181), channel_id=1, source_target_pairs={{0,4},{1,5},{2,6},{3,7},{4,8},{5,9},{6,10},{7,11},{8,12},{9,13},{1... | collective-permute-start | bytes 3145736 | tf_op jit(solution)/shard_map/ppermute | solution.py:161
  344.2 21.4 %collective-permute-start.30 = (bf16[512,1024]{0,1:T(8,128)(2,1)S(1)}, bf16[512,1024]{0,1:T(8,128)(2,1)}, u32[]{:S(2)}, u32[]{:S(2)}) collective-permute-start(bf16[512,1024]{0,1:T(8,128)(2,1)S(1)} %bitcast.182), channel_id=1, source_target_pairs={{4,0},{5,1},{6,2},{7,3},{8,4},{9,5},{10,6},{11,7},{12,8},{13,9},{1... | collective-permute-start | bytes 3145736 | tf_op jit(solution)/shard_map/ppermute | solution.py:161
  351.3 19.4 %collective-permute-start.27 = (bf16[2,128,2048]{2,1,0:T(8,128)(2,1)}, bf16[2,128,2048]{2,1,0:T(8,128)(2,1)}, u32[]{:S(2)}, u32[]{:S(2)}) collective-permute-start(bf16[2,128,2048]{2,1,0:T(8,128)(2,1)} %pad_maximum_fusion.10), channel_id=1, source_target_pairs={{0,1},{1,0},{2,3},{3,2},{4,5},{5,4},{6,7},{7,6},{8,9},{9,8},{10,11... | collective-permute-start | bytes 3145736 | tf_op jit(solution)/shard_map/ppermute | solution.py:14
  365.6 6.6 %collective-permute-start.31 = (bf16[512,1024]{0,1:T(8,128)(2,1)}, bf16[512,1024]{0,1:T(8,128)(2,1)}, u32[]{:S(2)}, u32[]{:S(2)}) collective-permute-start(bf16[512,1024]{0,1:T(8,128)(2,1)} %collective-permute-done.29), channel_id=1, source_target_pairs={{4,8},{5,9},{6,10},{7,11},{8,12},{9,13},{10,14},{11,15},{20,24},{2... | collective-permute-start | bytes 3145736 | tf_op jit(solution)/shard_map/ppermute | solution.py:161
  367.4 28.3 %collective-permute-start.32 = (bf16[512,1024]{0,1:T(8,128)(2,1)}, bf16[512,1024]{0,1:T(8,128)(2,1)}, u32[]{:S(2)}, u32[]{:S(2)}) collective-permute-start(bf16[512,1024]{0,1:T(8,128)(2,1)} %collective-permute-done.30), channel_id=1, source_target_pairs={{4,0},{5,1},{6,2},{7,3},{8,4},{9,5},{10,6},{11,7},{20,16},{21,17},... | collective-permute-start | bytes 3145736 | tf_op jit(solution)/shard_map/ppermute | solution.py:161
  368.6 66.4 %collective-permute-start.41 = (bf16[512,1024]{0,1:T(8,128)(2,1)}, bf16[512,1024]{0,1:T(8,128)(2,1)S(1)}, u32[]{:S(2)}, u32[]{:S(2)}) collective-permute-start(bf16[512,1024]{0,1:T(8,128)(2,1)} %copy-done.5), channel_id=1, source_target_pairs={{4,0},{5,1},{6,2},{7,3},{20,16},{21,17},{22,18},{23,19}} | collective-permute-start | bytes 3145736 | tf_op jit(solution)/shard_map/ppermute | solution.py:161
  369.9 72.4 %collective-permute-start.36 = (bf16[512,1024]{0,1:T(8,128)(2,1)S(1)}, bf16[512,1024]{0,1:T(8,128)(2,1)S(1)}, u32[]{:S(2)}, u32[]{:S(2)}) collective-permute-start(bf16[512,1024]{0,1:T(8,128)(2,1)S(1)} %collective-permute-done.25), channel_id=1, source_target_pairs={{8,12},{9,13},{10,14},{11,15},{24,28},{25,29},{26,30},{27,31}} | collective-permute-start | bytes 3145736 | tf_op jit(solution)/shard_map/ppermute | solution.py:161
  372.2 31.8 %copy-start.6 = (bf16[512,1024]{0,1:T(8,128)(2,1)S(1)}, bf16[512,1024]{0,1:T(8,128)(2,1)}, u32[]{:S(2)}) copy-start(bf16[512,1024]{0,1:T(8,128)(2,1)} %copy-done.5) | copy-start | bytes 3145732
  395.6 37.0 %collective-permute-start.42 = (bf16[512,1024]{0,1:T(8,128)(2,1)}, bf16[512,1024]{0,1:T(8,128)(2,1)S(1)}, u32[]{:S(2)}, u32[]{:S(2)}) collective-permute-start(bf16[512,1024]{0,1:T(8,128)(2,1)} %collective-permute-done.32), channel_id=1, source_target_pairs={{4,0},{5,1},{6,2},{7,3},{20,16},{21,17},{22,18},{23,19}} | collective-permute-start | bytes 3145736 | tf_op jit(solution)/shard_map/ppermute | solution.py:161
  396.9 41.8 %collective-permute-start.37 = (bf16[512,1024]{0,1:T(8,128)(2,1)}, bf16[512,1024]{0,1:T(8,128)(2,1)}, u32[]{:S(2)}, u32[]{:S(2)}) collective-permute-start(bf16[512,1024]{0,1:T(8,128)(2,1)} %collective-permute-done.31), channel_id=1, source_target_pairs={{8,12},{9,13},{10,14},{11,15},{24,28},{25,29},{26,30},{27,31}} | collective-permute-start | bytes 3145736 | tf_op jit(solution)/shard_map/ppermute | solution.py:161
  398.8 33.8 %slice-start.2 = ((s8[8388608]{0:T(1024)(128)(4,1)}), s8[4194304]{0:T(1024)(128)(4,1)S(1)}, s32[]{:S(2)}) async-start(s8[8388608]{0:T(1024)(128)(4,1)} %bitcast.153), calls=%async_computation.2 | async-start | bytes 8388608
  404.0 28.6 %slice-start.3 = ((s8[8388608]{0:T(1024)(128)(4,1)}), s8[4194304]{0:T(1024)(128)(4,1)S(1)}, s32[]{:S(2)}) async-start(s8[8388608]{0:T(1024)(128)(4,1)} %bitcast.153), calls=%async_computation.3 | async-start | bytes 8388608
  410.0 35.9 %collective-permute-start.33 = (bf16[2,128,2048]{2,1,0:T(8,128)(2,1)}, bf16[2,128,2048]{2,1,0:T(8,128)(2,1)S(1)}, u32[]{:S(2)}, u32[]{:S(2)}) collective-permute-start(bf16[2,128,2048]{2,1,0:T(8,128)(2,1)} %pad_maximum_fusion.11), channel_id=1, source_target_pairs={{0,1},{1,0},{2,3},{3,2},{4,5},{5,4},{6,7},{7,6},{8,9},{9,8},{10,11... | collective-permute-start | bytes 3145736 | tf_op jit(solution)/shard_map/ppermute | solution.py:14
  438.7 9.8 %collective-permute-start.43 = (bf16[2,128,2048]{2,1,0:T(8,128)(2,1)}, bf16[2,128,2048]{2,1,0:T(8,128)(2,1)S(1)}, u32[]{:S(2)}, u32[]{:S(2)}) collective-permute-start(bf16[2,128,2048]{2,1,0:T(8,128)(2,1)} %pad_maximum_fusion.13), channel_id=1, source_target_pairs={{0,1},{1,0},{2,3},{3,2},{4,5},{5,4},{6,7},{7,6},{8,9},{9,8},{10,11... | collective-permute-start | bytes 3145736 | tf_op jit(solution)/shard_map/ppermute | solution.py:14
  445.3 2.2 copy-start
  445.3 16.0 %collective-permute-start.38 = (bf16[2,128,2048]{2,1,0:T(8,128)(2,1)S(1)}, bf16[2,128,2048]{2,1,0:T(8,128)(2,1)S(1)}, u32[]{:S(2)}, u32[]{:S(2)}) collective-permute-start(bf16[2,128,2048]{2,1,0:T(8,128)(2,1)S(1)} %pad_maximum_fusion.12), channel_id=1, source_target_pairs={{0,1},{1,0},{2,3},{3,2},{4,5},{5,4},{6,7},{7,6},{8,9},{9,8},{10,11... | collective-permute-start | bytes 3145736 | tf_op jit(solution)/shard_map/ppermute | solution.py:14
  446.3 14.8 %collective-permute-start.34 = (bf16[128,2048]{1,0:T(8,128)(2,1)S(1)}, bf16[128,2048]{1,0:T(8,128)(2,1)S(1)}, u32[]{:S(2)}, u32[]{:S(2)}) collective-permute-start(bf16[128,2048]{1,0:T(8,128)(2,1)S(1)} %fusion.38), channel_id=1, source_target_pairs={{0,2},{1,3},{2,0},{3,1},{4,6},{5,7},{6,4},{7,5},{8,10},{9,11},{10,... | collective-permute-start | bytes 1572872 | tf_op jit(solution)/shard_map/ppermute | solution.py:14
  447.6 47.4 %collective-permute-start.28 = (bf16[128,2048]{1,0:T(8,128)(2,1)S(1)}, bf16[128,2048]{1,0:T(8,128)(2,1)S(1)}, u32[]{:S(2)}, u32[]{:S(2)}) collective-permute-start(bf16[128,2048]{1,0:T(8,128)(2,1)S(1)} %fusion.43), channel_id=1, source_target_pairs={{0,2},{1,3},{2,0},{3,1},{4,6},{5,7},{6,4},{7,5},{8,10},{9,11},{10,... | collective-permute-start | bytes 1572872 | tf_op jit(solution)/shard_map/ppermute | solution.py:14
  448.9 34.7 %collective-permute-start.44 = (bf16[128,2048]{1,0:T(8,128)(2,1)S(1)}, bf16[128,2048]{1,0:T(8,128)(2,1)S(1)}, u32[]{:S(2)}, u32[]{:S(2)}) collective-permute-start(bf16[128,2048]{1,0:T(8,128)(2,1)S(1)} %fusion.28), channel_id=1, source_target_pairs={{0,2},{1,3},{2,0},{3,1},{4,6},{5,7},{6,4},{7,5},{8,10},{9,11},{10,... | collective-permute-start | bytes 1572872 | tf_op jit(solution)/shard_map/ppermute | solution.py:14
  461.3 34.1 %collective-permute-start.35 = (bf16[128,2048]{1,0:T(8,128)(2,1)S(1)}, bf16[128,2048]{1,0:T(8,128)(2,1)S(1)}, u32[]{:S(2)}, u32[]{:S(2)}) collective-permute-start(bf16[128,2048]{1,0:T(8,128)(2,1)S(1)} %fusion.41), channel_id=1, source_target_pairs={{0,8},{1,9},{2,10},{3,11},{4,12},{5,13},{6,14},{7,15},{8,0},{9,1},... | collective-permute-start | bytes 1572872 | tf_op jit(solution)/shard_map/ppermute | solution.py:161
  461.7 32.2 %collective-permute-start.39 = (bf16[128,2048]{1,0:T(8,128)(2,1)S(1)}, bf16[128,2048]{1,0:T(8,128)(2,1)S(1)}, u32[]{:S(2)}, u32[]{:S(2)}) collective-permute-start(bf16[128,2048]{1,0:T(8,128)(2,1)S(1)} %fusion.33), channel_id=1, source_target_pairs={{0,2},{1,3},{2,0},{3,1},{4,6},{5,7},{6,4},{7,5},{8,10},{9,11},{10,... | collective-permute-start | bytes 1572872 | tf_op jit(solution)/shard_map/ppermute | solution.py:14
  483.8 25.2 %collective-permute-start.45 = (bf16[128,2048]{1,0:T(8,128)(2,1)S(1)}, bf16[128,2048]{1,0:T(8,128)(2,1)S(1)}, u32[]{:S(2)}, u32[]{:S(2)}) collective-permute-start(bf16[128,2048]{1,0:T(8,128)(2,1)S(1)} %fusion.31), channel_id=1, source_target_pairs={{0,12},{1,13},{2,14},{3,15},{4,0},{5,1},{6,2},{7,3},{8,4},{9,5},{1... | collective-permute-start | bytes 1572872 | tf_op jit(solution)/shard_map/ppermute | solution.py:161
  494.1 14.9 %collective-permute-start.40 = (bf16[128,2048]{1,0:T(8,128)(2,1)S(1)}, bf16[128,2048]{1,0:T(8,128)(2,1)S(1)}, u32[]{:S(2)}, u32[]{:S(2)}) collective-permute-start(bf16[128,2048]{1,0:T(8,128)(2,1)S(1)} %fusion.36), channel_id=1, source_target_pairs={{0,4},{1,5},{2,6},{3,7},{4,8},{5,9},{6,10},{7,11},{8,12},{9,13},{1... | collective-permute-start | bytes 1572872 | tf_op jit(solution)/shard_map/ppermute | solution.py:161
  509.0 1.3 copy-start.4

commit v3 on v2

--- a/solution.py
+++ b/solution.py
@@ -202,15 +202,20 @@
         widened * lax.rsqrt(jnp.mean(widened * widened, axis=1, keepdims=True) + 1e-05) * norm_gain
     ).astype(jnp.bfloat16)
 
-    slots = []
-    for r in range(ring):
-        start = (plane + r) % ring * depth
-        block = lax.dynamic_slice_in_dim(normed, start, depth, 1)
+    def beside(block):
+        pair = jnp.stack([block, partner_2(block, "mp", 1)])
+        other = partner_2(pair, "mp", 0)
+        return jnp.stack([pair[0], other[0], pair[1], other[1]]).reshape(rows, depth)
+
+    blocks = {}
+    for r in (0, 1, 3, 2):
+        block = lax.dynamic_slice_in_dim(normed, (plane + r) % ring * depth, depth, 1)
+        if r == 2:
+            block = lax.optimization_barrier((block, blocks[1], blocks[3]))[0]
         if r > 0:
             block = hop(block, [(z, (z + r) % ring) for z in range(ring)])
-        pair = jnp.stack([block, partner_2(block, "mp", 1)])
-        other = partner_2(pair, "mp", 0)
-        slots.append(jnp.stack([pair[0], other[0], pair[1], other[1]]).reshape(rows, depth))
+        blocks[r] = block
+    slots = {r: beside(blocks[r]) for r in (1, 3, 0)}
 
     order = [place ^ j for j in range(4)]
     positions = jnp.concatenate(
@@ -260,14 +265,48 @@
         queries = (queries * HEAD_SIZE ** (-0.5)).astype(jnp.bfloat16)
         return attention(queries, keys, values, allowed)
 
-    totals = [None] * ring
-    arrived, summed = {}, {}
+    def total(r):
+        result = None
+        for piece in range(PIECES):
+            block = from_left[piece][0]
+            if r > 0:
+                block = jnp.where(plane >= r, from_left[piece][r], from_right[piece][ring - r])
+            out_rows = output_tiles[piece * step : (piece + 1) * step]
+            product = jnp.dot(block, out_rows, preferred_element_type=jnp.float32)
+            result = product if result is None else result + product
+        return result.reshape(4, owned, depth)
+
+    def outgoing(four):
+        return jnp.stack([four[1], four[3]]).astype(jnp.bfloat16)
+
+    def over_core(four, away):
+        landed = partner_2(away, "mp", 0).astype(jnp.float32)
+        return four[0] + landed[0], (four[2] + landed[1]).astype(jnp.bfloat16)
+
+    def over_y(near, far):
+        return (near + partner_2(far, "mp", 1).astype(jnp.float32)).astype(jnp.bfloat16)
+
+    arrived, finished = {}, {}
+    attended = (ring - 1) * PIECES + 1
     from_left = [[] for _ in range(PIECES)]
     from_right = [[] for _ in range(PIECES)]
     hops = ring - 1
     for tick in range(1, hops * PIECES + 2 + hops):
         payloads, receivers = [], []
         attending = None
+        extra = []
+        if tick == 1:
+            extra = [blocks[2]]
+        elif tick == attended + 1:
+            first_four = total(0)
+            extra = [outgoing(first_four)]
+            for piece in range(PIECES - 1):
+                extra += [from_left[piece][hops], from_right[piece][hops]]
+        elif tick == attended + 2:
+            extra = [far]
+        elif tick == attended + 3:
+            middle_four = total(2)
+            extra = [outgoing(middle_four)]
         for piece in range(PIECES):
             k = tick - hops * piece
             if 1 <= k <= hops:
@@ -287,7 +326,20 @@
             if 1 <= k <= hops:
                 payloads += [from_left[piece][-1], from_right[piece][-1]]
                 receivers.append(("gather", piece, k))
-        payloads = list(lax.optimization_barrier(tuple(payloads)))
+        payloads = list(lax.optimization_barrier(tuple(extra + payloads)))
+        extra, payloads = payloads[: len(extra)], payloads[len(extra) :]
+        if tick == 1:
+            slots[2] = beside(extra[0])
+        elif tick == attended + 1:
+            near, far = over_core(first_four, extra[0])
+            for piece in range(PIECES - 1):
+                from_left[piece][hops], from_right[piece][hops] = extra[
+                    2 * piece + 1 : 2 * piece + 3
+                ]
+        elif tick == attended + 2:
+            finished[0] = over_y(near, extra[0])
+        elif tick == attended + 3:
+            finished[2] = over_y(*over_core(middle_four, extra[0]))
         if attending is not None:
             own = attend(attending, payloads.pop(0))
             from_left[attending].append(own)
@@ -299,25 +351,12 @@
             else:
                 from_left[piece].append(hop(first, right[k - 1 :]))
                 from_right[piece].append(hop(second, left[: ring - k]))
-    for r in range(ring):
-        for piece in range(PIECES):
-            block = from_left[piece][0]
-            if r > 0:
-                block = jnp.where(
-                    plane >= r, from_left[piece][r], from_right[piece][ring - r]
-                )
-            out_rows = output_tiles[piece * step : (piece + 1) * step]
-            product = jnp.dot(block, out_rows, preferred_element_type=jnp.float32)
-            totals[r] = product if totals[r] is None else totals[r] + product
-
     out = jnp.zeros((owned, width), jnp.bfloat16)
     for r in (0, 2, 3, 1):
-        four = totals[r].reshape(4, owned, depth)
-        away = jnp.stack([four[1], four[3]]).astype(jnp.bfloat16)
-        arrived = partner_2(away, "mp", 0).astype(jnp.float32)
-        far = (four[2] + arrived[1]).astype(jnp.bfloat16)
-        near = four[0] + arrived[0] + partner_2(far, "mp", 1).astype(jnp.float32)
-        block = near.astype(jnp.bfloat16)
+        block = finished.get(r)
+        if block is None:
+            four = total(r)
+            block = over_y(*over_core(four, outgoing(four)))
         if r > 0:
             block = hop(block, [(z, (z - r) % ring) for z in range(ring)])
         out = lax.dynamic_update_slice_in_dim(out, block, (plane + r) % ring * depth, 1)

time: 520 us -> 547 us (1.052)
  starting transfers between devices: 75.7 us -> 89.1 us
  other arithmetic: 20 us -> 28.9 us
    ppermute x16, waiting for transfers between devices: 54.8 us -> 43.4 us  [partner_2(): return lax.ppermute(value, axis, pairs)]
    ppermute x30, starting transfers between devices: 66.8 us -> 76.9 us  [hop(): return lax.ppermute(value, 'mp', full)]
    ppermute x30, waiting for transfers between devices: 277 us -> 283 us  [hop(): return lax.ppermute(value, 'mp', full)]
    unnamed x34 -> x100, local copies, waits for them, and re-layouts: 5.69 us -> 11.4 us
  transfers between devices with their start and end apart: 46 -> 46, of which waited for: 22 -> 24; matrix products, arithmetic and copies ran while one was open for 16% -> 16% of each run, Pallas kernels for 0% -> 0%
where the time goes in v3:
time: 547 us; the launch traced here: 539 us
  waiting for transfers between devices  327 us (60%)
  starting transfers between devices  89.1 us (16%)
  matrix products  67.5 us (12%)
  other arithmetic  28.9 us (5%)
  local copies, waits for them, and re-layouts  25 us (5%)
    ppermute x30, waiting for transfers between devices, hop(): return lax.ppermute(value, 'mp', full)  283 us
    ppermute x30, starting transfers between devices, hop(): return lax.ppermute(value, 'mp', full)  76.9 us
    ppermute x16, waiting for transfers between devices, partner_2(): return lax.ppermute(value, axis, pairs)  43.4 us
    dot_general x8, matrix products, total(): product = jnp.dot(block, out_rows, preferred_element_type=jnp.float32)  34 us
    dot_general x8, matrix products, part(): jnp.dot(slots[r], weights[piece], preferred_element_type=jnp.float32)  23.3 us
    ppermute x16, starting transfers between devices, partner_2(): return lax.ppermute(value, axis, pairs)  12.2 us
    unnamed x100, local copies, waits for them, and re-layouts  11.4 us
  transfers between devices with their start and end apart: 46, of which 24 were waited for; matrix products, arithmetic and copies ran while one was open for 16% of the time, Pallas kernels for 0%

profile of v3, /device:TPU:0, one launch (start us, length us, event | category | flops | bytes accessed | tf_op | source)
XLA Modules:
  0.0 538.7 jit_solution(12442957234777723230)
XLA Ops:
  0.0 2.2 fusion.2
  4.8 3.0 collective-permute-start.5
  9.4 2.2 collective-permute-start.2
  11.6 11.0 %collective-permute-done.5 = bf16[128,2048]{1,0:T(8,128)(2,1)S(1)} collective-permute-done((bf16[128,2048]{1,0:T(8,128)(2,1)S(1)}, bf16[128,2048]{1,0:T(8,128)(2,1)S(1)}, u32[]{:S(2)}, u32[]{:S(2)}) %collective-permute-start.5) | collective-permute-done | bytes 524320 | tf_op jit(solution)/shard_map/ppermute | solution.py:161
  22.7 1.8 collective-permute-start.7
  24.5 3.8 fusion.103
  28.3 4.8 collective-permute-done.2
  39.2 11.8 %collective-permute-start.6 = (bf16[128,2048]{1,0:T(8,128)(2,1)}, bf16[128,2048]{1,0:T(8,128)(2,1)}, u32[]{:S(2)}, u32[]{:S(2)}) collective-permute-start(bf16[128,2048]{1,0:T(8,128)(2,1)} %get-tuple-element.38), channel_id=1, source_target_pairs={{0,8},{1,9},{2,10},{3,11},{4,12},{5,13},{6,14},{7,15},{8,0},{9,1},... | collective-permute-start | bytes 1572872 | tf_op jit(solution)/shard_map/ppermute | solution.py:161
  53.0 2.6 copy-done.7
  55.6 2.9 fusion.100
  60.4 2.9 fusion.101
  66.0 8.7 %collective-permute-done.6 = bf16[128,2048]{1,0:T(8,128)(2,1)} collective-permute-done((bf16[128,2048]{1,0:T(8,128)(2,1)}, bf16[128,2048]{1,0:T(8,128)(2,1)}, u32[]{:S(2)}, u32[]{:S(2)}) %collective-permute-start.6) | collective-permute-done | bytes 524320 | tf_op jit(solution)/shard_map/ppermute | solution.py:161
  77.5 10.8 %collective-permute-done.9 = bf16[128,2048]{1,0:T(8,128)(2,1)} collective-permute-done((bf16[128,2048]{1,0:T(8,128)(2,1)}, bf16[128,2048]{1,0:T(8,128)(2,1)}, u32[]{:S(2)}, u32[]{:S(2)}) %collective-permute-start.9) | collective-permute-done | bytes 524320 | tf_op jit(solution)/shard_map/ppermute | solution.py:14
  93.3 2.7 collective-permute-start.11
  99.9 2.9 fusion.99
  102.8 21.8 %collective-permute-done.11 = bf16[512,1280]{1,0:T(8,128)(2,1)S(1)} collective-permute-done((bf16[512,1280]{1,0:T(8,128)(2,1)S(1)}, bf16[512,1280]{1,0:T(8,128)(2,1)S(1)}, u32[]{:S(2)}, u32[]{:S(2)}) %collective-permute-start.11) | collective-permute-done | bytes 1310752 | tf_op jit(solution)/shard_map/ppermute | solution.py:161
  125.9 2.9 fusion.102
  128.9 5.0 collective-permute-start.13
  133.9 2.9 fusion.98
  137.3 24.4 %collective-permute-done.13 = bf16[512,1280]{1,0:T(8,128)(2,1)S(1)} collective-permute-done((bf16[512,1280]{1,0:T(8,128)(2,1)S(1)}, bf16[512,1280]{1,0:T(8,128)(2,1)S(1)}, u32[]{:S(2)}, u32[]{:S(2)}) %collective-permute-start.13) | collective-permute-done | bytes 1310752 | tf_op jit(solution)/shard_map/ppermute | solution.py:161
  162.1 5.2 collective-permute-start.15
  168.6 2.9 fusion.97
  171.6 2.9 fusion.95
  174.5 19.9 %collective-permute-done.15 = bf16[512,1280]{1,0:T(8,128)(2,1)S(1)} collective-permute-done((bf16[512,1280]{1,0:T(8,128)(2,1)S(1)}, bf16[512,1280]{1,0:T(8,128)(2,1)S(1)}, u32[]{:S(2)}, u32[]{:S(2)}) %collective-permute-start.15) | collective-permute-done | bytes 1310752 | tf_op jit(solution)/shard_map/ppermute | solution.py:161
  194.4 4.9 collective-permute-done.16
  199.7 3.7 collective-permute-start.17
  203.5 9.3 %collective-permute-start.18 = (bf16[512,1280]{1,0:T(8,128)(2,1)S(1)}, bf16[512,1280]{1,0:T(8,128)(2,1)S(1)}, u32[]{:S(2)}, u32[]{:S(2)}) collective-permute-start(bf16[512,1280]{1,0:T(8,128)(2,1)S(1)} %convert_element_type.180), channel_id=1, source_target_pairs={{12,8},{13,9},{14,10},{15,11},{28,24},{29,25},{30,26},{31,27}} | collective-permute-start | bytes 3932168 | tf_op jit(solution)/shard_map/ppermute | solution.py:161
  216.1 2.4 fusion
  218.6 2.1 fusion.22
  220.7 8.7 %collective-permute-done.17 = bf16[512,1280]{1,0:T(8,128)(2,1)S(1)} collective-permute-done((bf16[512,1280]{1,0:T(8,128)(2,1)S(1)}, bf16[512,1280]{1,0:T(8,128)(2,1)S(1)}, u32[]{:S(2)}, u32[]{:S(2)}) %collective-permute-start.17) | collective-permute-done | bytes 1310752 | tf_op jit(solution)/shard_map/ppermute | solution.py:161
  230.7 5.0 collective-permute-start.21
  235.7 4.5 collective-permute-start.19
  241.9 23.0 %collective-permute-done.21 = bf16[512,1280]{1,0:T(8,128)(2,1)S(1)} collective-permute-done((bf16[512,1280]{1,0:T(8,128)(2,1)S(1)}, bf16[512,1280]{1,0:T(8,128)(2,1)S(1)}, u32[]{:S(2)}, u32[]{:S(2)}) %collective-permute-start.21) | collective-permute-done | bytes 1310752 | tf_op jit(solution)/shard_map/ppermute | solution.py:161
  265.2 18.1 %collective-permute-done.19 = bf16[512,1024]{0,1:T(8,128)(2,1)S(1)} collective-permute-done((bf16[512,1024]{0,1:T(8,128)(2,1)S(1)}, bf16[512,1024]{0,1:T(8,128)(2,1)S(1)}, u32[]{:S(2)}, u32[]{:S(2)}) %collective-permute-start.19) | collective-permute-done | bytes 1048608 | tf_op jit(solution)/shard_map/ppermute | solution.py:161
  283.2 4.5 collective-permute-start.23
  289.0 2.9 fusion.96
  292.7 1.7 collective-permute-start.26
  294.4 2.4 fusion.17
  296.8 15.0 %collective-permute-done.23 = bf16[512,1280]{1,0:T(8,128)(2,1)S(1)} collective-permute-done((bf16[512,1280]{1,0:T(8,128)(2,1)S(1)}, bf16[512,1280]{1,0:T(8,128)(2,1)S(1)}, u32[]{:S(2)}, u32[]{:S(2)}) %collective-permute-start.23) | collective-permute-done | bytes 1310752 | tf_op jit(solution)/shard_map/ppermute | solution.py:161
  311.8 9.8 %collective-permute-done.24 = bf16[512,1280]{1,0:T(8,128)(2,1)S(1)} collective-permute-done((bf16[512,1280]{1,0:T(8,128)(2,1)S(1)}, bf16[512,1280]{1,0:T(8,128)(2,1)S(1)}, u32[]{:S(2)}, u32[]{:S(2)}) %collective-permute-start.24) | collective-permute-done | bytes 1310752 | tf_op jit(solution)/shard_map/ppermute | solution.py:161
  322.1 16.7 %collective-permute-done.26 = bf16[512,1024]{0,1:T(8,128)(2,1)S(1)} collective-permute-done((bf16[512,1024]{0,1:T(8,128)(2,1)S(1)}, bf16[512,1024]{0,1:T(8,128)(2,1)S(1)}, u32[]{:S(2)}, u32[]{:S(2)}) %collective-permute-start.26) | collective-permute-done | bytes 1048608 | tf_op jit(solution)/shard_map/ppermute | solution.py:161
  344.2 2.5 fusion.1
  346.7 3.1 fusion.21
  349.8 3.7 fusion.112
  353.7 10.2 %collective-permute-done.28 = bf16[512,1024]{0,1:T(8,128)(2,1)S(1)} collective-permute-done((bf16[512,1024]{0,1:T(8,128)(2,1)S(1)}, bf16[512,1024]{0,1:T(8,128)(2,1)S(1)}, u32[]{:S(2)}, u32[]{:S(2)}) %collective-permute-start.28) | collective-permute-done | bytes 1048608 | tf_op jit(solution)/shard_map/ppermute | solution.py:161
  364.0 2.4 collective-permute-start.30
  369.0 19.9 %collective-permute-done.30 = bf16[512,1024]{0,1:T(8,128)(2,1)} collective-permute-done((bf16[512,1024]{0,1:T(8,128)(2,1)}, bf16[512,1024]{0,1:T(8,128)(2,1)}, u32[]{:S(2)}, u32[]{:S(2)}) %collective-permute-start.30) | collective-permute-done | bytes 1048608 | tf_op jit(solution)/shard_map/ppermute | solution.py:161
  388.9 5.2 collective-permute-done.31
  394.2 1.6 collective-permute-start.33
  397.1 25.5 %collective-permute-done.34 = bf16[512,1024]{0,1:T(8,128)(2,1)} collective-permute-done((bf16[512,1024]{0,1:T(8,128)(2,1)}, bf16[512,1024]{0,1:T(8,128)(2,1)}, u32[]{:S(2)}, u32[]{:S(2)}) %collective-permute-start.34) | collective-permute-done | bytes 1048608 | tf_op jit(solution)/shard_map/ppermute | solution.py:161
  422.6 5.0 fusion.11
  427.6 6.8 %fusion.113 = (bf16[512,2048]{1,0:T(8,128)(2,1)S(1)}, f32[512,2048]{1,0:T(8,128)}) fusion(f32[512,2048]{1,0:T(8,128)S(1)} %fusion.11, bf16[2048,2048]{1,0:T(8,128)(2,1)} %param.13, bf16[512,1024]{0,1:T(8,128)(2,1)S(1)} %copy-done.27, bf16[512,1024]{0,1:T(8,128)(2,1)S(1)} %copy-done.29, pred[]{:T(512)S(6)} %ge.12), kind=kOutput, calls=%fused_computation.194 | convolution fusion | flops 2150105088 | bytes 16777216 | tf_op jit(solution)/shard_map/dot_general | solution.py:275
  437.8 23.6 %collective-permute-done.42 = bf16[512,1024]{0,1:T(8,128)(2,1)} collective-permute-done((bf16[512,1024]{0,1:T(8,128)(2,1)}, bf16[512,1024]{0,1:T(8,128)(2,1)}, u32[]{:S(2)}, u32[]{:S(2)}) %collective-permute-start.42) | collective-permute-done | bytes 1048608 | tf_op jit(solution)/shard_map/ppermute | solution.py:161
  461.5 5.1 fusion.7
  466.7 4.9 fusion.115
  475.1 1.8 collective-permute-start.36
  476.9 3.7 fusion.9
  480.6 2.5 fusion.114
  484.7 1.8 collective-permute-start.44
  486.5 3.8 collective-permute-done.36
  492.0 1.8 collective-permute-start.40
  493.8 18.8 %collective-permute-done.44 = bf16[128,2048]{1,0:T(8,128)(2,1)S(1)} collective-permute-done((bf16[128,2048]{1,0:T(8,128)(2,1)S(1)}, bf16[128,2048]{1,0:T(8,128)(2,1)S(1)}, u32[]{:S(2)}, u32[]{:S(2)}) %collective-permute-start.44) | collective-permute-done | bytes 524320 | tf_op jit(solution)/shard_map/ppermute | solution.py:14
  512.9 9.2 %collective-permute-done.40 = bf16[128,2048]{1,0:T(8,128)(2,1)S(1)} collective-permute-done((bf16[128,2048]{1,0:T(8,128)(2,1)S(1)}, bf16[128,2048]{1,0:T(8,128)(2,1)S(1)}, u32[]{:S(2)}, u32[]{:S(2)}) %collective-permute-start.40) | collective-permute-done | bytes 524320 | tf_op jit(solution)/shard_map/ppermute | solution.py:14
  524.1 12.2 %collective-permute-done.41 = bf16[128,2048]{1,0:T(8,128)(2,1)S(1)} collective-permute-done((bf16[128,2048]{1,0:T(8,128)(2,1)S(1)}, bf16[128,2048]{1,0:T(8,128)(2,1)S(1)}, u32[]{:S(2)}, u32[]{:S(2)}) %collective-permute-start.41) | collective-permute-done | bytes 524320 | tf_op jit(solution)/shard_map/ppermute | solution.py:161
  (219 shorter events, 65.2 us)
Async XLA Ops:
  2.3 22.2 %copy-start.4 = (bf16[2048,2048]{1,0:T(8,128)(2,1)S(1)}, bf16[2048,2048]{1,0:T(8,128)(2,1)}, u32[]{:S(2)}) copy-start(bf16[2048,2048]{1,0:T(8,128)(2,1)} %param.10) | copy-start | bytes 25165828
  4.8 17.8 %collective-permute-start.5 = (bf16[128,2048]{1,0:T(8,128)(2,1)S(1)}, bf16[128,2048]{1,0:T(8,128)(2,1)S(1)}, u32[]{:S(2)}, u32[]{:S(2)}) collective-permute-start(bf16[128,2048]{1,0:T(8,128)(2,1)S(1)} %get-tuple-element.98), channel_id=1, source_target_pairs={{0,4},{1,5},{2,6},{3,7},{4,8},{5,9},{6,10},{7,11},{8,12},{9,13},{1... | collective-permute-start | bytes 1572872 | tf_op jit(solution)/shard_map/ppermute | solution.py:161
  7.9 29.7 %collective-permute-start = (bf16[128,2048]{1,0:T(8,128)(2,1)S(1)}, bf16[128,2048]{1,0:T(8,128)(2,1)S(1)}, u32[]{:S(2)}, u32[]{:S(2)}) collective-permute-start(bf16[128,2048]{1,0:T(8,128)(2,1)S(1)} %get-tuple-element.97), channel_id=1, source_target_pairs={{0,2},{1,3},{2,0},{3,1},{4,6},{5,7},{6,4},{7,5},{8,10},{9,11},{10,... | collective-permute-start | bytes 1572872 | tf_op jit(solution)/shard_map/ppermute | solution.py:14
  9.4 23.7 %collective-permute-start.2 = (bf16[128,2048]{1,0:T(8,128)(2,1)S(1)}, bf16[128,2048]{1,0:T(8,128)(2,1)S(1)}, u32[]{:S(2)}, u32[]{:S(2)}) collective-permute-start(bf16[128,2048]{1,0:T(8,128)(2,1)S(1)} %get-tuple-element.100), channel_id=1, source_target_pairs={{0,12},{1,13},{2,14},{3,15},{4,0},{5,1},{6,2},{7,3},{8,4},{9,5},{1... | collective-permute-start | bytes 1572872 | tf_op jit(solution)/shard_map/ppermute | solution.py:161
  22.7 12.3 %collective-permute-start.7 = (bf16[128,2048]{1,0:T(8,128)(2,1)S(1)}, bf16[128,2048]{1,0:T(8,128)(2,1)S(1)}, u32[]{:S(2)}, u32[]{:S(2)}) collective-permute-start(bf16[128,2048]{1,0:T(8,128)(2,1)S(1)} %collective-permute-done.5), channel_id=1, source_target_pairs={{0,2},{1,3},{2,0},{3,1},{4,6},{5,7},{6,4},{7,5},{8,10},{9,11},{10,... | collective-permute-start | bytes 1572872 | tf_op jit(solution)/shard_map/ppermute | solution.py:14
  33.1 18.0 %copy-start.16 = (bf16[128,2048]{1,0:T(8,128)(2,1)}, bf16[128,2048]{1,0:T(8,128)(2,1)S(1)}, u32[]{:S(2)}) copy-start(bf16[128,2048]{1,0:T(8,128)(2,1)S(1)} %collective-permute-done.2) | copy-start | bytes 1572868
  33.1 18.0 %collective-permute-start.3 = (bf16[128,2048]{1,0:T(8,128)(2,1)S(1)}, bf16[128,2048]{1,0:T(8,128)(2,1)S(1)}, u32[]{:S(2)}, u32[]{:S(2)}) collective-permute-start(bf16[128,2048]{1,0:T(8,128)(2,1)S(1)} %collective-permute-done.2), channel_id=1, source_target_pairs={{0,2},{1,3},{2,0},{3,1},{4,6},{5,7},{6,4},{7,5},{8,10},{9,11},{10,... | collective-permute-start | bytes 1572872 | tf_op jit(solution)/shard_map/ppermute | solution.py:14
  36.0 15.2 %collective-permute-start.8 = (bf16[2,128,2048]{2,1,0:T(8,128)(2,1)}, bf16[2,128,2048]{2,1,0:T(8,128)(2,1)}, u32[]{:S(2)}, u32[]{:S(2)}) collective-permute-start(bf16[2,128,2048]{2,1,0:T(8,128)(2,1)} %pad_maximum_fusion.8), channel_id=1, source_target_pairs={{0,1},{1,0},{2,3},{3,2},{4,5},{5,4},{6,7},{7,6},{8,9},{9,8},{10,11... | collective-permute-start | bytes 3145736 | tf_op jit(solution)/shard_map/ppermute | solution.py:14
  37.6 15.1 %copy-start.14 = (bf16[128,2048]{1,0:T(8,128)(2,1)}, bf16[128,2048]{1,0:T(8,128)(2,1)S(1)}, u32[]{:S(2)}) copy-start(bf16[128,2048]{1,0:T(8,128)(2,1)S(1)} %collective-permute-done) | copy-start | bytes 1572868
  38.7 51.9 %collective-permute-start.1 = (bf16[2,128,2048]{2,1,0:T(8,128)(2,1)}, bf16[2,128,2048]{2,1,0:T(8,128)(2,1)}, u32[]{:S(2)}, u32[]{:S(2)}) collective-permute-start(bf16[2,128,2048]{2,1,0:T(8,128)(2,1)} %pad_maximum_fusion.6), channel_id=1, source_target_pairs={{0,1},{1,0},{2,3},{3,2},{4,5},{5,4},{6,7},{7,6},{8,9},{9,8},{10,11... | collective-permute-start | bytes 3145736 | tf_op jit(solution)/shard_map/ppermute | solution.py:14
  39.2 35.4 %collective-permute-start.6 = (bf16[128,2048]{1,0:T(8,128)(2,1)}, bf16[128,2048]{1,0:T(8,128)(2,1)}, u32[]{:S(2)}, u32[]{:S(2)}) collective-permute-start(bf16[128,2048]{1,0:T(8,128)(2,1)} %get-tuple-element.38), channel_id=1, source_target_pairs={{0,8},{1,9},{2,10},{3,11},{4,12},{5,13},{6,14},{7,15},{8,0},{9,1},... | collective-permute-start | bytes 1572872 | tf_op jit(solution)/shard_map/ppermute | solution.py:161
  51.2 8.6 %collective-permute-start.4 = (bf16[2,128,2048]{2,1,0:T(8,128)(2,1)S(1)}, bf16[2,128,2048]{2,1,0:T(8,128)(2,1)S(1)}, u32[]{:S(2)}, u32[]{:S(2)}) collective-permute-start(bf16[2,128,2048]{2,1,0:T(8,128)(2,1)S(1)} %pad_maximum_fusion.7), channel_id=1, source_target_pairs={{0,1},{1,0},{2,3},{3,2},{4,5},{5,4},{6,7},{7,6},{8,9},{9,8},{10,11... | collective-permute-start | bytes 3145736 | tf_op jit(solution)/shard_map/ppermute | solution.py:14
  74.7 13.6 %collective-permute-start.9 = (bf16[128,2048]{1,0:T(8,128)(2,1)}, bf16[128,2048]{1,0:T(8,128)(2,1)}, u32[]{:S(2)}, u32[]{:S(2)}) collective-permute-start(bf16[128,2048]{1,0:T(8,128)(2,1)} %collective-permute-done.6), channel_id=1, source_target_pairs={{0,2},{1,3},{2,0},{3,1},{4,6},{5,7},{6,4},{7,5},{8,10},{9,11},{10,... | collective-permute-start | bytes 1572872 | tf_op jit(solution)/shard_map/ppermute | solution.py:14
  76.0 16.0 %copy-start.15 = (bf16[128,2048]{1,0:T(8,128)(2,1)S(1)}, bf16[128,2048]{1,0:T(8,128)(2,1)}, u32[]{:S(2)}) copy-start(bf16[128,2048]{1,0:T(8,128)(2,1)} %copy-done.14) | copy-start | bytes 1572868
  89.6 7.4 %collective-permute-start.10 = (bf16[2,128,2048]{2,1,0:T(8,128)(2,1)S(1)}, bf16[2,128,2048]{2,1,0:T(8,128)(2,1)S(1)}, u32[]{:S(2)}, u32[]{:S(2)}) collective-permute-start(bf16[2,128,2048]{2,1,0:T(8,128)(2,1)S(1)} %pad_maximum_fusion.9), channel_id=1, source_target_pairs={{0,1},{1,0},{2,3},{3,2},{4,5},{5,4},{6,7},{7,6},{8,9},{9,8},{10,11... | collective-permute-start | bytes 3145736 | tf_op jit(solution)/shard_map/ppermute | solution.py:14
  93.3 31.3 %collective-permute-start.11 = (bf16[512,1280]{1,0:T(8,128)(2,1)S(1)}, bf16[512,1280]{1,0:T(8,128)(2,1)S(1)}, u32[]{:S(2)}, u32[]{:S(2)}) collective-permute-start(bf16[512,1280]{1,0:T(8,128)(2,1)S(1)} %copy-done.20), channel_id=1, source_target_pairs={{0,4},{1,5},{2,6},{3,7},{16,20},{17,21},{18,22},{19,23}} | collective-permute-start | bytes 3932168 | tf_op jit(solution)/shard_map/ppermute | solution.py:161
  96.0 28.6 %collective-permute-start.12 = (bf16[512,1280]{1,0:T(8,128)(2,1)S(1)}, bf16[512,1280]{1,0:T(8,128)(2,1)S(1)}, u32[]{:S(2)}, u32[]{:S(2)}) collective-permute-start(bf16[512,1280]{1,0:T(8,128)(2,1)S(1)} %copy-done.21), channel_id=1, source_target_pairs={{12,8},{13,9},{14,10},{15,11},{28,24},{29,25},{30,26},{31,27}} | collective-permute-start | bytes 3932168 | tf_op jit(solution)/shard_map/ppermute | solution.py:161
  125.1 11.9 %collective-permute-start.14 = (bf16[512,1280]{1,0:T(8,128)(2,1)S(1)}, bf16[512,1280]{1,0:T(8,128)(2,1)S(1)}, u32[]{:S(2)}, u32[]{:S(2)}) collective-permute-start(bf16[512,1280]{1,0:T(8,128)(2,1)S(1)} %get-tuple-element.43), channel_id=1, source_target_pairs={{8,4},{9,5},{10,6},{11,7},{12,8},{13,9},{14,10},{15,11},{24,20},{2... | collective-permute-start | bytes 3932168 | tf_op jit(solution)/shard_map/ppermute | solution.py:161
  128.9 32.8 %collective-permute-start.13 = (bf16[512,1280]{1,0:T(8,128)(2,1)S(1)}, bf16[512,1280]{1,0:T(8,128)(2,1)S(1)}, u32[]{:S(2)}, u32[]{:S(2)}) collective-permute-start(bf16[512,1280]{1,0:T(8,128)(2,1)S(1)} %get-tuple-element.42), channel_id=1, source_target_pairs={{0,4},{1,5},{2,6},{3,7},{4,8},{5,9},{6,10},{7,11},{16,20},{17,21},... | collective-permute-start | bytes 3932168 | tf_op jit(solution)/shard_map/ppermute | solution.py:161
  137.0 24.7 %copy-start.1 = (f32[512,1280]{1,0:T(8,128)S(1)}, f32[512,1280]{1,0:T(8,128)}, u32[]{:S(2)}) copy-start(f32[512,1280]{1,0:T(8,128)} %copy-done) | copy-start | bytes 7864324
  137.3 31.3 %copy-start.11 = (bf16[4,128,2048]{2,1,0:T(8,128)(2,1)S(1)}, bf16[4,128,2048]{2,1,0:T(8,128)(2,1)}, u32[]{:S(2)}) copy-start(bf16[4,128,2048]{2,1,0:T(8,128)(2,1)} %copy-done.10) | copy-start | bytes 6291460
  162.1 32.3 %collective-permute-start.15 = (bf16[512,1280]{1,0:T(8,128)(2,1)S(1)}, bf16[512,1280]{1,0:T(8,128)(2,1)S(1)}, u32[]{:S(2)}, u32[]{:S(2)}) collective-permute-start(bf16[512,1280]{1,0:T(8,128)(2,1)S(1)} %add_convert_fusion.5), channel_id=1, source_target_pairs={{0,4},{1,5},{2,6},{3,7},{4,8},{5,9},{6,10},{7,11},{8,12},{9,13},{1... | collective-permute-start | bytes 3932168 | tf_op jit(solution)/shard_map/ppermute | solution.py:161
  167.2 32.0 %collective-permute-start.16 = (bf16[512,1280]{1,0:T(8,128)(2,1)S(1)}, bf16[512,1280]{1,0:T(8,128)(2,1)S(1)}, u32[]{:S(2)}, u32[]{:S(2)}) collective-permute-start(bf16[512,1280]{1,0:T(8,128)(2,1)S(1)} %add_convert_fusion.4), channel_id=1, source_target_pairs={{4,0},{5,1},{6,2},{7,3},{8,4},{9,5},{10,6},{11,7},{12,8},{13,9},{1... | collective-permute-start | bytes 3932168 | tf_op jit(solution)/shard_map/ppermute | solution.py:161
  199.7 29.7 %collective-permute-start.17 = (bf16[512,1280]{1,0:T(8,128)(2,1)S(1)}, bf16[512,1280]{1,0:T(8,128)(2,1)S(1)}, u32[]{:S(2)}, u32[]{:S(2)}) collective-permute-start(bf16[512,1280]{1,0:T(8,128)(2,1)S(1)} %convert_element_type.179), channel_id=1, source_target_pairs={{0,4},{1,5},{2,6},{3,7},{16,20},{17,21},{18,22},{19,23}} | collective-permute-start | bytes 3932168 | tf_op jit(solution)/shard_map/ppermute | solution.py:161
  203.5 26.0 %collective-permute-start.18 = (bf16[512,1280]{1,0:T(8,128)(2,1)S(1)}, bf16[512,1280]{1,0:T(8,128)(2,1)S(1)}, u32[]{:S(2)}, u32[]{:S(2)}) collective-permute-start(bf16[512,1280]{1,0:T(8,128)(2,1)S(1)} %convert_element_type.180), channel_id=1, source_target_pairs={{12,8},{13,9},{14,10},{15,11},{28,24},{29,25},{30,26},{31,27}} | collective-permute-start | bytes 3932168 | tf_op jit(solution)/shard_map/ppermute | solution.py:161
  230.0 11.6 %collective-permute-start.22 = (bf16[512,1280]{1,0:T(8,128)(2,1)S(1)}, bf16[512,1280]{1,0:T(8,128)(2,1)S(1)}, u32[]{:S(2)}, u32[]{:S(2)}) collective-permute-start(bf16[512,1280]{1,0:T(8,128)(2,1)S(1)} %get-tuple-element.52), channel_id=1, source_target_pairs={{8,4},{9,5},{10,6},{11,7},{12,8},{13,9},{14,10},{15,11},{24,20},{2... | collective-permute-start | bytes 3932168 | tf_op jit(solution)/shard_map/ppermute | solution.py:161
  230.7 34.2 %collective-permute-start.21 = (bf16[512,1280]{1,0:T(8,128)(2,1)S(1)}, bf16[512,1280]{1,0:T(8,128)(2,1)S(1)}, u32[]{:S(2)}, u32[]{:S(2)}) collective-permute-start(bf16[512,1280]{1,0:T(8,128)(2,1)S(1)} %get-tuple-element.51), channel_id=1, source_target_pairs={{0,4},{1,5},{2,6},{3,7},{4,8},{5,9},{6,10},{7,11},{16,20},{17,21},... | collective-permute-start | bytes 3932168 | tf_op jit(solution)/shard_map/ppermute | solution.py:161
  235.7 47.5 %collective-permute-start.19 = (bf16[512,1024]{0,1:T(8,128)(2,1)S(1)}, bf16[512,1024]{0,1:T(8,128)(2,1)S(1)}, u32[]{:S(2)}, u32[]{:S(2)}) collective-permute-start(bf16[512,1024]{0,1:T(8,128)(2,1)S(1)} %bitcast.177), channel_id=1, source_target_pairs={{0,4},{1,5},{2,6},{3,7},{4,8},{5,9},{6,10},{7,11},{8,12},{9,13},{1... | collective-permute-start | bytes 3145736 | tf_op jit(solution)/shard_map/ppermute | solution.py:161
  240.3 43.0 %collective-permute-start.20 = (bf16[512,1024]{0,1:T(8,128)(2,1)S(1)}, bf16[512,1024]{0,1:T(8,128)(2,1)S(1)}, u32[]{:S(2)}, u32[]{:S(2)}) collective-permute-start(bf16[512,1024]{0,1:T(8,128)(2,1)S(1)} %bitcast.178), channel_id=1, source_target_pairs={{4,0},{5,1},{6,2},{7,3},{8,4},{9,5},{10,6},{11,7},{12,8},{13,9},{1... | collective-permute-start | bytes 3145736 | tf_op jit(solution)/shard_map/ppermute | solution.py:161
  241.8 47.2 %copy-start.36 = (bf16[2048,128]{1,0:T(8,128)(2,1)S(1)}, bf16[2048,128]{1,0:T(8,128)(2,1)}, u32[]{:S(2)}) copy-start(bf16[2048,128]{1,0:T(8,128)(2,1)} %get-tuple-element.101) | copy-start | bytes 1572868
  241.9 47.2 %copy-start.38 = (bf16[2048,128]{1,0:T(8,128)(2,1)S(1)}, bf16[2048,128]{1,0:T(8,128)(2,1)}, u32[]{:S(2)}) copy-start(bf16[2048,128]{1,0:T(8,128)(2,1)} %get-tuple-element.132) | copy-start | bytes 1572868
  264.9 29.5 %slice-start = ((s8[8388608]{0:T(1024)(128)(4,1)}), s8[4194304]{0:T(1024)(128)(4,1)S(1)}, s32[]{:S(2)}) async-start(s8[8388608]{0:T(1024)(128)(4,1)} %bitcast.151), calls=%async_computation | async-start | bytes 8388608
  265.1 29.3 %slice-start.1 = ((s8[8388608]{0:T(1024)(128)(4,1)}), s8[4194304]{0:T(1024)(128)(4,1)S(1)}, s32[]{:S(2)}) async-start(s8[8388608]{0:T(1024)(128)(4,1)} %bitcast.151), calls=%async_computation.1 | async-start | bytes 8388608
  283.2 28.6 %collective-permute-start.23 = (bf16[512,1280]{1,0:T(8,128)(2,1)S(1)}, bf16[512,1280]{1,0:T(8,128)(2,1)S(1)}, u32[]{:S(2)}, u32[]{:S(2)}) collective-permute-start(bf16[512,1280]{1,0:T(8,128)(2,1)S(1)} %add_convert_fusion.1), channel_id=1, source_target_pairs={{0,4},{1,5},{2,6},{3,7},{4,8},{5,9},{6,10},{7,11},{8,12},{9,13},{1... | collective-permute-start | bytes 3932168 | tf_op jit(solution)/shard_map/ppermute | solution.py:161
  287.7 33.9 %collective-permute-start.24 = (bf16[512,1280]{1,0:T(8,128)(2,1)S(1)}, bf16[512,1280]{1,0:T(8,128)(2,1)S(1)}, u32[]{:S(2)}, u32[]{:S(2)}) collective-permute-start(bf16[512,1280]{1,0:T(8,128)(2,1)S(1)} %add_convert_fusion), channel_id=1, source_target_pairs={{4,0},{5,1},{6,2},{7,3},{8,4},{9,5},{10,6},{11,7},{12,8},{13,9},{1... | collective-permute-start | bytes 3932168 | tf_op jit(solution)/shard_map/ppermute | solution.py:161
  292.0 30.1 %collective-permute-start.25 = (bf16[512,1024]{0,1:T(8,128)(2,1)S(1)}, bf16[512,1024]{0,1:T(8,128)(2,1)S(1)}, u32[]{:S(2)}, u32[]{:S(2)}) collective-permute-start(bf16[512,1024]{0,1:T(8,128)(2,1)S(1)} %collective-permute-done.19), channel_id=1, source_target_pairs={{4,8},{5,9},{6,10},{7,11},{8,12},{9,13},{10,14},{11,15},{20,24},{2... | collective-permute-start | bytes 3145736 | tf_op jit(solution)/shard_map/ppermute | solution.py:161
  292.7 46.1 %collective-permute-start.26 = (bf16[512,1024]{0,1:T(8,128)(2,1)S(1)}, bf16[512,1024]{0,1:T(8,128)(2,1)S(1)}, u32[]{:S(2)}, u32[]{:S(2)}) collective-permute-start(bf16[512,1024]{0,1:T(8,128)(2,1)S(1)} %collective-permute-done.20), channel_id=1, source_target_pairs={{4,0},{5,1},{6,2},{7,3},{8,4},{9,5},{10,6},{11,7},{20,16},{21,17},... | collective-permute-start | bytes 3145736 | tf_op jit(solution)/shard_map/ppermute | solution.py:161
  322.1 19.4 %copy-start.26 = (bf16[512,1024]{0,1:T(8,128)(2,1)}, bf16[512,1024]{0,1:T(8,128)(2,1)S(1)}, u32[]{:S(2)}) copy-start(bf16[512,1024]{0,1:T(8,128)(2,1)S(1)} %collective-permute-done.25) | copy-start | bytes 3145732
  341.4 12.3 %collective-permute-start.27 = (bf16[512,1024]{0,1:T(8,128)(2,1)S(1)}, bf16[512,1024]{0,1:T(8,128)(2,1)S(1)}, u32[]{:S(2)}, u32[]{:S(2)}) collective-permute-start(bf16[512,1024]{0,1:T(8,128)(2,1)S(1)} %collective-permute-done.25), channel_id=1, source_target_pairs={{8,12},{9,13},{10,14},{11,15},{24,28},{25,29},{26,30},{27,31}} | collective-permute-start | bytes 3145736 | tf_op jit(solution)/shard_map/ppermute | solution.py:161
  342.2 21.8 %collective-permute-start.28 = (bf16[512,1024]{0,1:T(8,128)(2,1)S(1)}, bf16[512,1024]{0,1:T(8,128)(2,1)S(1)}, u32[]{:S(2)}, u32[]{:S(2)}) collective-permute-start(bf16[512,1024]{0,1:T(8,128)(2,1)S(1)} %collective-permute-done.26), channel_id=1, source_target_pairs={{4,0},{5,1},{6,2},{7,3},{20,16},{21,17},{22,18},{23,19}} | collective-permute-start | bytes 3145736 | tf_op jit(solution)/shard_map/ppermute | solution.py:161
  353.5 14.6 %copy-start.3 = (f32[512,2048]{1,0:T(8,128)}, f32[512,2048]{1,0:T(8,128)S(1)}, u32[]{:S(2)}) copy-start(f32[512,2048]{1,0:T(8,128)S(1)} %get-tuple-element.124) | copy-start | bytes 12582916
  353.7 15.3 %copy-start.24 = (bf16[512,1024]{0,1:T(8,128)(2,1)}, bf16[512,1024]{0,1:T(8,128)(2,1)S(1)}, u32[]{:S(2)}) copy-start(bf16[512,1024]{0,1:T(8,128)(2,1)S(1)} %collective-permute-done.27) | copy-start | bytes 3145732
  364.0 3.9 collective-permute-start.29
  364.0 25.0 %collective-permute-start.30 = (bf16[512,1024]{0,1:T(8,128)(2,1)}, bf16[512,1024]{0,1:T(8,128)(2,1)}, u32[]{:S(2)}, u32[]{:S(2)}) collective-permute-start(bf16[512,1024]{0,1:T(8,128)(2,1)} %bitcast.27), channel_id=1, source_target_pairs={{0,4},{1,5},{2,6},{3,7},{4,8},{5,9},{6,10},{7,11},{8,12},{9,13},{1... | collective-permute-start | bytes 3145736 | tf_op jit(solution)/shard_map/ppermute | solution.py:161
  366.4 27.8 %collective-permute-start.31 = (bf16[512,1024]{0,1:T(8,128)(2,1)}, bf16[512,1024]{0,1:T(8,128)(2,1)}, u32[]{:S(2)}, u32[]{:S(2)}) collective-permute-start(bf16[512,1024]{0,1:T(8,128)(2,1)} %bitcast.27), channel_id=1, source_target_pairs={{4,0},{5,1},{6,2},{7,3},{8,4},{9,5},{10,6},{11,7},{12,8},{13,9},{1... | collective-permute-start | bytes 3145736 | tf_op jit(solution)/shard_map/ppermute | solution.py:161
  394.2 2.9 collective-permute-start.33
  395.8 26.8 %collective-permute-start.34 = (bf16[512,1024]{0,1:T(8,128)(2,1)}, bf16[512,1024]{0,1:T(8,128)(2,1)}, u32[]{:S(2)}, u32[]{:S(2)}) collective-permute-start(bf16[512,1024]{0,1:T(8,128)(2,1)} %collective-permute-done.31), channel_id=1, source_target_pairs={{4,0},{5,1},{6,2},{7,3},{8,4},{9,5},{10,6},{11,7},{20,16},{21,17},... | collective-permute-start | bytes 3145736 | tf_op jit(solution)/shard_map/ppermute | solution.py:161
  397.1 30.5 %copy-start.27 = (bf16[512,1024]{0,1:T(8,128)(2,1)S(1)}, bf16[512,1024]{0,1:T(8,128)(2,1)}, u32[]{:S(2)}) copy-start(bf16[512,1024]{0,1:T(8,128)(2,1)} %copy-done.26) | copy-start | bytes 3145732
  397.1 30.5 %copy-start.29 = (bf16[512,1024]{0,1:T(8,128)(2,1)S(1)}, bf16[512,1024]{0,1:T(8,128)(2,1)}, u32[]{:S(2)}) copy-start(bf16[512,1024]{0,1:T(8,128)(2,1)} %copy-done.28) | copy-start | bytes 3145732
  435.6 25.9 %collective-permute-start.42 = (bf16[512,1024]{0,1:T(8,128)(2,1)}, bf16[512,1024]{0,1:T(8,128)(2,1)}, u32[]{:S(2)}, u32[]{:S(2)}) collective-permute-start(bf16[512,1024]{0,1:T(8,128)(2,1)} %collective-permute-done.34), channel_id=1, source_target_pairs={{4,0},{5,1},{6,2},{7,3},{20,16},{21,17},{22,18},{23,19}} | collective-permute-start | bytes 3145736 | tf_op jit(solution)/shard_map/ppermute | solution.py:161
  436.9 29.8 %copy-start.23 = (bf16[512,1024]{0,1:T(8,128)(2,1)S(1)}, bf16[512,1024]{0,1:T(8,128)(2,1)}, u32[]{:S(2)}) copy-start(bf16[512,1024]{0,1:T(8,128)(2,1)} %copy-done.22) | copy-start | bytes 3145732
  436.9 29.8 %copy-start.31 = (bf16[512,1024]{0,1:T(8,128)(2,1)S(1)}, bf16[512,1024]{0,1:T(8,128)(2,1)}, u32[]{:S(2)}) copy-start(bf16[512,1024]{0,1:T(8,128)(2,1)} %copy-done.30) | copy-start | bytes 3145732
  436.9 40.0 %collective-permute-start.38 = (bf16[512,1024]{0,1:T(8,128)(2,1)}, bf16[512,1024]{0,1:T(8,128)(2,1)S(1)}, u32[]{:S(2)}, u32[]{:S(2)}) collective-permute-start(bf16[512,1024]{0,1:T(8,128)(2,1)} %collective-permute-done.33), channel_id=1, source_target_pairs={{8,12},{9,13},{10,14},{11,15},{24,28},{25,29},{26,30},{27,31}} | collective-permute-start | bytes 3145736 | tf_op jit(solution)/shard_map/ppermute | solution.py:161
  437.8 35.0 %collective-permute-start.35 = (bf16[2,128,2048]{2,1,0:T(8,128)(2,1)}, bf16[2,128,2048]{2,1,0:T(8,128)(2,1)S(1)}, u32[]{:S(2)}, u32[]{:S(2)}) collective-permute-start(bf16[2,128,2048]{2,1,0:T(8,128)(2,1)} %pad_maximum_fusion.11), channel_id=1, source_target_pairs={{0,1},{1,0},{2,3},{3,2},{4,5},{5,4},{6,7},{7,6},{8,9},{9,8},{10,11... | collective-permute-start | bytes 3145736 | tf_op jit(solution)/shard_map/ppermute | solution.py:14
  461.5 15.4 %slice-start.2 = ((s8[8388608]{0:T(1024)(128)(4,1)}), s8[4194304]{0:T(1024)(128)(4,1)S(1)}, s32[]{:S(2)}) async-start(s8[8388608]{0:T(1024)(128)(4,1)} %bitcast.153), calls=%async_computation.2 | async-start | bytes 8388608
  472.7 11.7 %collective-permute-start.43 = (bf16[2,128,2048]{2,1,0:T(8,128)(2,1)}, bf16[2,128,2048]{2,1,0:T(8,128)(2,1)S(1)}, u32[]{:S(2)}, u32[]{:S(2)}) collective-permute-start(bf16[2,128,2048]{2,1,0:T(8,128)(2,1)} %pad_maximum_fusion.13), channel_id=1, source_target_pairs={{0,1},{1,0},{2,3},{3,2},{4,5},{5,4},{6,7},{7,6},{8,9},{9,8},{10,11... | collective-permute-start | bytes 3145736 | tf_op jit(solution)/shard_map/ppermute | solution.py:14
  475.1 15.2 %collective-permute-start.36 = (bf16[128,2048]{1,0:T(8,128)(2,1)}, bf16[128,2048]{1,0:T(8,128)(2,1)}, u32[]{:S(2)}, u32[]{:S(2)}) collective-permute-start(bf16[128,2048]{1,0:T(8,128)(2,1)} %fusion.38), channel_id=1, source_target_pairs={{0,2},{1,3},{2,0},{3,1},{4,6},{5,7},{6,4},{7,5},{8,10},{9,11},{10,... | collective-permute-start | bytes 1572872 | tf_op jit(solution)/shard_map/ppermute | solution.py:14
  483.2 8.4 %collective-permute-start.39 = (bf16[2,128,2048]{2,1,0:T(8,128)(2,1)S(1)}, bf16[2,128,2048]{2,1,0:T(8,128)(2,1)S(1)}, u32[]{:S(2)}, u32[]{:S(2)}) collective-permute-start(bf16[2,128,2048]{2,1,0:T(8,128)(2,1)S(1)} %pad_maximum_fusion.12), channel_id=1, source_target_pairs={{0,1},{1,0},{2,3},{3,2},{4,5},{5,4},{6,7},{7,6},{8,9},{9,8},{10,11... | collective-permute-start | bytes 3145736 | tf_op jit(solution)/shard_map/ppermute | solution.py:14
  484.1 38.3 %collective-permute-start.32 = (bf16[128,2048]{1,0:T(8,128)(2,1)S(1)}, bf16[128,2048]{1,0:T(8,128)(2,1)S(1)}, u32[]{:S(2)}, u32[]{:S(2)}) collective-permute-start(bf16[128,2048]{1,0:T(8,128)(2,1)S(1)} %copy-done.34), channel_id=1, source_target_pairs={{0,2},{1,3},{2,0},{3,1},{4,6},{5,7},{6,4},{7,5},{8,10},{9,11},{10,... | collective-permute-start | bytes 1572872 | tf_op jit(solution)/shard_map/ppermute | solution.py:14
  484.7 27.9 %collective-permute-start.44 = (bf16[128,2048]{1,0:T(8,128)(2,1)S(1)}, bf16[128,2048]{1,0:T(8,128)(2,1)S(1)}, u32[]{:S(2)}, u32[]{:S(2)}) collective-permute-start(bf16[128,2048]{1,0:T(8,128)(2,1)S(1)} %fusion.28), channel_id=1, source_target_pairs={{0,2},{1,3},{2,0},{3,1},{4,6},{5,7},{6,4},{7,5},{8,10},{9,11},{10,... | collective-permute-start | bytes 1572872 | tf_op jit(solution)/shard_map/ppermute | solution.py:14
  491.5 32.5 %collective-permute-start.37 = (bf16[128,2048]{1,0:T(8,128)(2,1)S(1)}, bf16[128,2048]{1,0:T(8,128)(2,1)S(1)}, u32[]{:S(2)}, u32[]{:S(2)}) collective-permute-start(bf16[128,2048]{1,0:T(8,128)(2,1)S(1)} %fusion.41), channel_id=1, source_target_pairs={{0,8},{1,9},{2,10},{3,11},{4,12},{5,13},{6,14},{7,15},{8,0},{9,1},... | collective-permute-start | bytes 1572872 | tf_op jit(solution)/shard_map/ppermute | solution.py:161
  492.0 30.1 %collective-permute-start.40 = (bf16[128,2048]{1,0:T(8,128)(2,1)S(1)}, bf16[128,2048]{1,0:T(8,128)(2,1)S(1)}, u32[]{:S(2)}, u32[]{:S(2)}) collective-permute-start(bf16[128,2048]{1,0:T(8,128)(2,1)S(1)} %fusion.33), channel_id=1, source_target_pairs={{0,2},{1,3},{2,0},{3,1},{4,6},{5,7},{6,4},{7,5},{8,10},{9,11},{10,... | collective-permute-start | bytes 1572872 | tf_op jit(solution)/shard_map/ppermute | solution.py:14
  512.8 23.6 %collective-permute-start.45 = (bf16[128,2048]{1,0:T(8,128)(2,1)S(1)}, bf16[128,2048]{1,0:T(8,128)(2,1)S(1)}, u32[]{:S(2)}, u32[]{:S(2)}) collective-permute-start(bf16[128,2048]{1,0:T(8,128)(2,1)S(1)} %fusion.31), channel_id=1, source_target_pairs={{0,12},{1,13},{2,14},{3,15},{4,0},{5,1},{6,2},{7,3},{8,4},{9,5},{1... | collective-permute-start | bytes 1572872 | tf_op jit(solution)/shard_map/ppermute | solution.py:161
  522.3 14.0 %collective-permute-start.41 = (bf16[128,2048]{1,0:T(8,128)(2,1)S(1)}, bf16[128,2048]{1,0:T(8,128)(2,1)S(1)}, u32[]{:S(2)}, u32[]{:S(2)}) collective-permute-start(bf16[128,2048]{1,0:T(8,128)(2,1)S(1)} %fusion.36), channel_id=1, source_target_pairs={{0,4},{1,5},{2,6},{3,7},{4,8},{5,9},{6,10},{7,11},{8,12},{9,13},{1... | collective-permute-start | bytes 1572872 | tf_op jit(solution)/shard_map/ppermute | solution.py:161
  (30 other events, 131.6 us)
